TPU v7x, 256 devices: a whole 4x4x8 slice. The times are simulated.
256 devices in a mesh: section: 4 (over y), tp: 16 (over z, core), dp: 4 (over x).
Axes of the slice: x: 4, y: 4, z: 8, core: 2. Of those that a mesh axis runs over, the one named last changes fastest.
Arguments:
- rollout_acts: bfloat16 [8192, 1024], P('tp', 'dp'), may hold values from -6 to 6
- pack_source: int32 [4, 2, 128], P('dp'), may hold values from 0 to 1023, as said below
- segments: int32 [4, 2, 128], P('dp'), may hold values from 0 to 31, as said below
- gain: bfloat16 [4, 8192], P('section', 'tp'), may hold values from 0.25 to 1.75
- wq: bfloat16 [4, 8192, 4096], P('section', None, 'tp'), may hold values from -0.0625 to 0.0625
- wkv: bfloat16 [4, 2, 8192, 1024], P('section', None, None, 'tp'), may hold values from -0.0625 to 0.0625
- wo: bfloat16 [4, 4096, 8192], P('section', 'tp'), may hold values from -0.125 to 0.125
Outputs:
- layer_out: bfloat16 [4, 4, 2, 8192, 128], P('section', 'dp', None, 'tp')
- stash: bfloat16 [4, 4, 2, 8192, 128], P('section', 'dp', None, 'tp')
Inputs may be any that keep to these rules, and one draw needn't show every extreme that they name: `pack_source`: every rollout token appears at exactly one packed position. `segments`: ids never fall along a row; equal ids mark the tokens of one rollout, in order; rollouts may continue from one row into the next.
All inputs are finite; a program needn't handle non-finite values.
Results may differ from a plain program's by a relative error of at most 0.03.
Values may be sent and summed in bfloat16 or wider, within the bound.
No kernel may reach another device: no remote copies, remote signals or barrier semaphores. Data moves between devices by JAX's collectives and lax.ppermute only.
A program may use at most 64 MiB of HBM per device.

v0:
```python
import jax
import jax.numpy as jnp
from jax import lax
from jax.sharding import PartitionSpec as P

KV_HEADS = 8
HD = 128
MICRO = 2


EPS = 1e-05


def passed_along(block, axis, distance):
    devices = range(lax.axis_size(axis))
    route = [(i - distance, i) for i in devices if i - distance in devices]
    return lax.ppermute(block, axis, route)


def swapped(value, axis, bit):
    mask = 2**bit
    pairs = [(source, source ^ mask) for source in range(lax.axis_size(axis))]
    return lax.ppermute(value, axis, pairs)


def attention_layer(current, seg_ids, gain_rows, query_weight, kv_weight, out_weight):
    local_rows, seq_len = current.shape
    query_cols = query_weight.shape[1]
    local_heads = query_cols // HD
    contract = (((0,), (0,)), ((), ()))
    whole, whole_gain = (
        lax.all_gather(current, "tp", axis=0, tiled=True),
        lax.all_gather(gain_rows, "tp", axis=0, tiled=True),
    )
    widened = whole.astype(jnp.float32)
    mean_sq = jnp.mean(widened * widened, axis=0)
    normed = (
        widened * lax.rsqrt(mean_sq + EPS)[None, :] * whole_gain.astype(jnp.float32)[:, None]
    ).astype(jnp.bfloat16)
    queries = lax.dot_general(query_weight, normed, contract, preferred_element_type=jnp.float32)
    keyvals = jnp.einsum("cdk,ds->cks", kv_weight, normed, preferred_element_type=jnp.float32)
    queries = queries.astype(jnp.bfloat16).reshape(local_heads, HD, seq_len)
    kv_all = lax.all_gather(keyvals.astype(jnp.bfloat16), "tp", axis=1, tiled=True).reshape(
        2, KV_HEADS, HD, seq_len
    )
    head_ids = lax.axis_index("tp") * local_heads + jnp.arange(local_heads, dtype=jnp.int32)
    kv_ids = head_ids % KV_HEADS
    key_rows = jnp.take(kv_all[0], kv_ids, axis=0)
    value_rows = jnp.take(kv_all[1], kv_ids, axis=0)
    scores = jnp.einsum(
        "hdi,hdj->hij", queries, key_rows, preferred_element_type=jnp.float32
    ) * HD ** (-0.5)
    positions = jnp.arange(seq_len, dtype=jnp.int32)
    allowed = (seg_ids[:, None] == seg_ids[None, :]) & (positions[None, :] <= positions[:, None])
    weights = jnp.where(allowed[None], jnp.exp(jnp.where(allowed[None], scores, 0.0)), 0.0)
    probs = (weights / jnp.sum(weights, axis=-1, keepdims=True)).astype(jnp.bfloat16)
    mixed = jnp.einsum("hij,hdj->hdi", probs, value_rows, preferred_element_type=jnp.float32)
    mixed = mixed.astype(jnp.bfloat16).reshape(query_cols, seq_len)
    branch = lax.psum_scatter(
        lax.dot_general(out_weight, mixed, contract, preferred_element_type=jnp.float32).astype(
            jnp.bfloat16
        ),
        "tp",
        scatter_dimension=0,
        tiled=True,
    ).astype(jnp.float32)
    return (current.astype(jnp.float32) + branch).astype(jnp.bfloat16)


def shards(rollout_acts, pack_source, segments, gain, wq, wkv, wo):
    gathered = lax.all_gather(rollout_acts, "dp", axis=1, tiled=True)
    local_rows = gathered.shape[0]
    seq_len = segments.shape[2]
    packed = jnp.take(gathered, pack_source[0].reshape(-1), axis=1).reshape(
        local_rows, MICRO, seq_len
    )
    section_idx = lax.axis_index("section")
    section_count = lax.axis_size("section")
    clocks = MICRO + section_count - 1
    received = jnp.zeros((local_rows, seq_len), jnp.bfloat16)
    produced = jnp.zeros((MICRO, local_rows, seq_len), jnp.bfloat16)
    taken = jnp.zeros((MICRO, local_rows, seq_len), jnp.bfloat16)
    for clock in range(clocks):
        micro_idx = clock - section_idx
        active = (micro_idx >= 0) & (micro_idx < MICRO)
        which = jnp.clip(micro_idx, 0, MICRO - 1)
        current = jnp.where(section_idx == 0, packed[:, min(clock, MICRO - 1)], received)
        seg_ids = lax.dynamic_index_in_dim(segments[0], which, 0, keepdims=False)
        result = attention_layer(current, seg_ids, gain[0], wq[0], wkv[0], wo[0])
        produced = jnp.where(
            active, lax.dynamic_update_index_in_dim(produced, result, which, 0), produced
        )
        taken = jnp.where(active, lax.dynamic_update_index_in_dim(taken, current, which, 0), taken)
        if clock + 1 < clocks:
            received = passed_along(result, "section", 1)
    mirrored = taken
    for bit_pos in range(section_count.bit_length() - 1):
        mirrored = swapped(mirrored, "section", bit_pos)
    return (produced[None, None], mirrored[None, None])


def solution(mesh):
    in_specs = (
        P("tp", "dp"),
        P("dp", None, None),
        P("dp", None, None),
        P("section", "tp"),
        P("section", None, "tp"),
        P("section", None, None, "tp"),
        P("section", "tp", None),
    )
    out_specs = (P("section", "dp", None, "tp", None), P("section", "dp", None, "tp", None))
    return jax.shard_map(shards, mesh=mesh, in_specs=in_specs, out_specs=out_specs, check_vma=False)
```

profile of v0, /device:TPU:2, one launch (start us, length us, event | category | flops | bytes accessed | tf_op | source)
XLA Modules:
  0.0 733.4 jit_solution(16137093278697416367)
XLA Ops:
  7.2 1.9 copy.27
  10.6 28.4 %all-gather.9.cloned.1.call-done = bf16[512,1024]{0,1:T(8,128)(2,1)} async-done(((bf16[512,256]{0,1:T(8,128)(2,1)}), bf16[512,1024]{0,1:T(8,128)(2,1)}) %all-gather.9.cloned.1.call-update) | async-done | bytes 1048592 | tf_op jit(solution)/shard_map/all_gather | solution.py:71
  39.0 2.6 gather_fusion
  42.5 17.5 %all-gather.1 = bf16[1,8192]{1,0:T(2,128)(2,1)S(1)} all-gather(bf16[1,512]{1,0:T(2,128)(2,1)S(1)} %copy-done.12), channel_id=3, replica_groups=mesh['section'=4,'tp'=16,'dp'=4] {'tp'}, dimensions={1}, use_global_device_ids=true | all-gather | bytes 17408 | tf_op jit(solution)/shard_map/all_gather | solution.py:33
  60.3 23.4 %all-gather.19.cloned.1.call-done = bf16[8192,1,128]{0,2,1:T(8,128)(2,1)} async-done(((bf16[512,1,128]{0,2,1:T(8,128)(2,1)}), bf16[8192,1,128]{0,2,1:T(8,128)(2,1)}) %all-gather.19.cloned.1.call-update) | async-done | bytes 2097168 | tf_op jit(solution)/shard_map/all_gather | solution.py:32
  83.6 2.1 fusion.17
  85.7 3.6 fusion.77
  89.4 2.4 fusion.81
  91.9 17.1 %all_gather.43 = bf16[2,1024,128]{2,1,0:T(8,128)(2,1)S(1)} all-gather(bf16[2,64,128]{2,1,0:T(8,128)(2,1)S(1)} %convert_bitcast_fusion.4), channel_id=1, replica_groups=mesh['section'=4,'tp'=16,'dp'=4] {'tp'}, dimensions={1}, use_global_device_ids=true | all-gather | bytes 557056 | tf_op jit(solution)/shard_map/all_gather | solution.py:43
  110.7 4.3 fusion
  115.1 58.8 %reduce-scatter.6.cloned.1.call-done = bf16[512,128]{0,1:T(8,128)(2,1)} async-done(((bf16[8192,128]{0,1:T(8,128)(2,1)}), bf16[512,128]{0,1:T(8,128)(2,1)}) %reduce-scatter.6.cloned.1.call-update) | async-done | bytes 131088 | tf_op jit(solution)/shard_map/reduce_scatter | solution.py:59
  173.9 1.0 bitcast_dynamic-update-slice_fusion.1
  174.9 3.4 collective-permute-start
  178.3 2.5 collective-permute-done
  180.8 0.7 fusion.103
  181.6 0.7 fusion.129
  182.3 38.5 %all-gather.11.cloned.1.call-done = bf16[8192,128]{0,1:T(8,128)(2,1)} async-done(((bf16[512,128]{0,1:T(8,128)(2,1)}), bf16[8192,128]{0,1:T(8,128)(2,1)}) %all-gather.11.cloned.1.call-update) | async-done | bytes 2097168 | tf_op jit(solution)/shard_map/all_gather | solution.py:32
  220.8 2.1 fusion.5
  222.9 3.6 fusion.74
  226.7 2.4 fusion.93
  229.1 17.1 %all_gather.45 = bf16[2,1024,128]{2,1,0:T(8,128)(2,1)S(1)} all-gather(bf16[2,64,128]{2,1,0:T(8,128)(2,1)S(1)} %convert_bitcast_fusion.3), channel_id=1, replica_groups=mesh['section'=4,'tp'=16,'dp'=4] {'tp'}, dimensions={1}, use_global_device_ids=true | all-gather | bytes 557056 | tf_op jit(solution)/shard_map/all_gather | solution.py:43
  247.4 1.0 fusion.40
  248.7 4.3 fusion.1
  253.0 58.6 %reduce-scatter.8.cloned.1.call-done = bf16[512,128]{0,1:T(8,128)(2,1)} async-done(((bf16[8192,128]{0,1:T(8,128)(2,1)}), bf16[512,128]{0,1:T(8,128)(2,1)}) %reduce-scatter.8.cloned.1.call-update) | async-done | bytes 131088 | tf_op jit(solution)/shard_map/reduce_scatter | solution.py:59
  311.7 1.0 fusion.106
  312.6 3.6 collective-permute-start.1
  316.2 2.5 collective-permute-done.1
  319.5 39.3 %all-gather.13.cloned.1.call-done = bf16[8192,128]{0,1:T(8,128)(2,1)} async-done(((bf16[512,128]{0,1:T(8,128)(2,1)}), bf16[8192,128]{0,1:T(8,128)(2,1)}) %all-gather.13.cloned.1.call-update) | async-done | bytes 2097168 | tf_op jit(solution)/shard_map/all_gather | solution.py:32
  358.8 2.1 fusion.8
  360.9 3.6 fusion.71
  364.6 2.4 fusion.90
  367.1 17.3 %all_gather.47 = bf16[2,1024,128]{2,1,0:T(8,128)(2,1)S(1)} all-gather(bf16[2,64,128]{2,1,0:T(8,128)(2,1)S(1)} %convert_bitcast_fusion.2), channel_id=1, replica_groups=mesh['section'=4,'tp'=16,'dp'=4] {'tp'}, dimensions={1}, use_global_device_ids=true | all-gather | bytes 557056 | tf_op jit(solution)/shard_map/all_gather | solution.py:43
  385.6 1.0 fusion.43
  386.8 4.3 fusion.2
  391.2 58.6 %reduce-scatter.10.cloned.1.call-done = bf16[512,128]{0,1:T(8,128)(2,1)} async-done(((bf16[8192,128]{0,1:T(8,128)(2,1)}), bf16[512,128]{0,1:T(8,128)(2,1)}) %reduce-scatter.10.cloned.1.call-update) | async-done | bytes 131088 | tf_op jit(solution)/shard_map/reduce_scatter | solution.py:59
  449.8 1.0 fusion.105
  450.8 3.4 collective-permute-start.2
  454.2 2.5 collective-permute-done.2
  457.5 0.7 fusion.127
  458.2 38.8 %all-gather.15.cloned.1.call-done = bf16[8192,128]{0,1:T(8,128)(2,1)} async-done(((bf16[512,128]{0,1:T(8,128)(2,1)}), bf16[8192,128]{0,1:T(8,128)(2,1)}) %all-gather.15.cloned.1.call-update) | async-done | bytes 2097168 | tf_op jit(solution)/shard_map/all_gather | solution.py:32
  497.0 2.1 fusion.11
  499.1 3.6 fusion.68
  502.8 2.4 fusion.87
  505.2 17.1 %all_gather.49 = bf16[2,1024,128]{2,1,0:T(8,128)(2,1)S(1)} all-gather(bf16[2,64,128]{2,1,0:T(8,128)(2,1)S(1)} %convert_bitcast_fusion.1), channel_id=1, replica_groups=mesh['section'=4,'tp'=16,'dp'=4] {'tp'}, dimensions={1}, use_global_device_ids=true | all-gather | bytes 557056 | tf_op jit(solution)/shard_map/all_gather | solution.py:43
  523.5 1.0 fusion.46
  524.8 4.3 fusion.3
  529.2 58.8 %reduce-scatter.12.cloned.1.call-done = bf16[512,128]{0,1:T(8,128)(2,1)} async-done(((bf16[8192,128]{0,1:T(8,128)(2,1)}), bf16[512,128]{0,1:T(8,128)(2,1)}) %reduce-scatter.12.cloned.1.call-update) | async-done | bytes 131088 | tf_op jit(solution)/shard_map/reduce_scatter | solution.py:59
  588.0 1.0 fusion.104
  588.9 3.4 collective-permute-start.3
  592.3 2.5 collective-permute-done.3
  595.6 39.3 %all-gather.17.cloned.1.call-done = bf16[8192,128]{0,1:T(8,128)(2,1)} async-done(((bf16[512,128]{0,1:T(8,128)(2,1)}), bf16[8192,128]{0,1:T(8,128)(2,1)}) %all-gather.17.cloned.1.call-update) | async-done | bytes 2097168 | tf_op jit(solution)/shard_map/all_gather | solution.py:32
  634.9 2.1 fusion.14
  637.0 3.6 fusion.65
  640.7 2.4 fusion.84
  643.2 17.1 %all_gather.51 = bf16[2,1024,128]{2,1,0:T(8,128)(2,1)S(1)} all-gather(bf16[2,64,128]{2,1,0:T(8,128)(2,1)S(1)} %convert_bitcast_fusion), channel_id=1, replica_groups=mesh['section'=4,'tp'=16,'dp'=4] {'tp'}, dimensions={1}, use_global_device_ids=true | all-gather | bytes 557056 | tf_op jit(solution)/shard_map/all_gather | solution.py:43
  662.0 4.3 fusion.4
  666.4 1.6 collective-permute-start.4
  668.0 7.1 collective-permute-done.4
  675.0 3.0 collective-permute-start.5
  678.1 6.2 collective-permute-done.5
  684.3 0.8 copy.49
  685.1 39.9 %reduce-scatter.14.cloned.1.call-done = bf16[512,128]{0,1:T(8,128)(2,1)} async-done(((bf16[8192,128]{0,1:T(8,128)(2,1)}), bf16[512,128]{0,1:T(8,128)(2,1)}) %reduce-scatter.14.cloned.1.call-update) | async-done | bytes 131088 | tf_op jit(solution)/shard_map/reduce_scatter | solution.py:59
  725.1 1.0 fusion.99
  726.0 0.8 copy.48
  (102 shorter events, 13.3 us)
Async XLA Ops:
  7.2 82.3 %copy-start = (bf16[1,2,8192,64]{2,3,1,0:T(8,128)(2,1)S(1)}, bf16[1,2,8192,64]{2,3,1,0:T(8,128)(2,1)}, u32[]{:S(2)}) copy-start(bf16[1,2,8192,64]{2,3,1,0:T(8,128)(2,1)} %param.14) | copy-start | bytes 6291460
  7.2 35.3 %copy-start.12 = (bf16[1,512]{1,0:T(2,128)(2,1)S(1)}, bf16[1,512]{1,0:T(2,128)(2,1)}, u32[]{:S(2)}) copy-start(bf16[1,512]{1,0:T(2,128)(2,1)} %param.12) | copy-start | bytes 3076
  7.2 52.9 %copy-start.11 = (s32[1,2,128]{2,1,0:T(2,128)S(1)}, s32[1,2,128]{2,1,0:T(2,128)}, u32[]{:S(2)}) copy-start(s32[1,2,128]{2,1,0:T(2,128)} %param.11) | copy-start | bytes 3076
  7.2 31.8 %all-gather.9.cloned.1.call-start = ((), (), s32[]{:S(2)}) async-start(), calls=%async_computation.5 | async-start | bytes 1310720 | tf_op jit(solution)/shard_map/all_gather | solution.py:71
  9.2 74.4 %all-gather.19.cloned.1.call-start = ((), (), s32[]{:S(2)}) async-start(), calls=%async_computation.15 | async-start | bytes 2228224 | tf_op jit(solution)/shard_map/all_gather | solution.py:32
  42.4 131.5 %reduce-scatter.6.cloned.1.call-start = ((), (), s32[]{:S(2)}) async-start(), calls=%async_computation.6 | async-start | bytes 2228224 | tf_op jit(solution)/shard_map/reduce_scatter | solution.py:59
  60.1 166.6 %copy-start.6 = (f32[1,8192]{1,0:T(1,128)}, f32[1,8192]{1,0:T(1,128)S(1)}, u32[]{:S(2)}) copy-start(f32[1,8192]{1,0:T(1,128)S(1)} %convert_element_type.270) | copy-start | bytes 98308
  110.7 63.2 %copy-start.4 = (bf16[512,1,128]{0,2,1:T(8,128)(2,1)S(1)}, bf16[512,1,128]{0,2,1:T(8,128)(2,1)}, u32[]{:S(2)}) copy-start(bf16[512,1,128]{0,2,1:T(8,128)(2,1)} %get-tuple-element.16) | copy-start | bytes 393220
  115.1 105.8 %all-gather.11.cloned.1.call-start = ((), (), s32[]{:S(2)}) async-start(), calls=%async_computation.7 | async-start | bytes 2228224 | tf_op jit(solution)/shard_map/all_gather | solution.py:32
  174.9 5.9 collective-permute-start
  181.5 130.1 %reduce-scatter.8.cloned.1.call-start = ((), (), s32[]{:S(2)}) async-start(), calls=%async_computation.8 | async-start | bytes 2228224 | tf_op jit(solution)/shard_map/reduce_scatter | solution.py:59
  248.6 63.0 %copy-start.2 = (bf16[512,128]{0,1:T(8,128)(2,1)S(1)}, bf16[512,128]{0,1:T(8,128)(2,1)}, u32[]{:S(2)}) copy-start(bf16[512,128]{0,1:T(8,128)(2,1)} %get-tuple-element.14) | copy-start | bytes 393220
  253.0 107.9 %copy-start.7 = (f32[1,8192]{1,0:T(1,128)S(1)}, f32[1,8192]{1,0:T(1,128)}, u32[]{:S(2)}) copy-start(f32[1,8192]{1,0:T(1,128)} %copy-done.6) | copy-start | bytes 98308
  253.0 105.8 %all-gather.13.cloned.1.call-start = ((), (), s32[]{:S(2)}) async-start(), calls=%async_computation.9 | async-start | bytes 2228224 | tf_op jit(solution)/shard_map/all_gather | solution.py:32
  312.6 6.1 collective-permute-start.1
  319.4 130.4 %reduce-scatter.10.cloned.1.call-start = ((), (), s32[]{:S(2)}) async-start(), calls=%async_computation.10 | async-start | bytes 2228224 | tf_op jit(solution)/shard_map/reduce_scatter | solution.py:59
  386.8 63.0 %copy-start.3 = (bf16[512,128]{0,1:T(8,128)(2,1)S(1)}, bf16[512,128]{0,1:T(8,128)(2,1)}, u32[]{:S(2)}) copy-start(bf16[512,128]{0,1:T(8,128)(2,1)} %get-tuple-element.12) | copy-start | bytes 393220
  391.1 107.9 %copy-start.8 = (f32[1,8192]{1,0:T(1,128)S(1)}, f32[1,8192]{1,0:T(1,128)}, u32[]{:S(2)}) copy-start(f32[1,8192]{1,0:T(1,128)} %copy-done.6) | copy-start | bytes 98308
  391.2 105.8 %all-gather.15.cloned.1.call-start = ((), (), s32[]{:S(2)}) async-start(), calls=%async_computation.11 | async-start | bytes 2228224 | tf_op jit(solution)/shard_map/all_gather | solution.py:32
  450.8 5.9 collective-permute-start.2
  457.4 130.5 %reduce-scatter.12.cloned.1.call-start = ((), (), s32[]{:S(2)}) async-start(), calls=%async_computation.12 | async-start | bytes 2228224 | tf_op jit(solution)/shard_map/reduce_scatter | solution.py:59
  524.8 63.2 %copy-start.1 = (bf16[512,128]{0,1:T(8,128)(2,1)S(1)}, bf16[512,128]{0,1:T(8,128)(2,1)}, u32[]{:S(2)}) copy-start(bf16[512,128]{0,1:T(8,128)(2,1)} %get-tuple-element.10) | copy-start | bytes 393220
  529.1 107.9 %copy-start.9 = (f32[1,8192]{1,0:T(1,128)S(1)}, f32[1,8192]{1,0:T(1,128)}, u32[]{:S(2)}) copy-start(f32[1,8192]{1,0:T(1,128)} %copy-done.6) | copy-start | bytes 98308
  529.1 105.8 %all-gather.17.cloned.1.call-start = ((), (), s32[]{:S(2)}) async-start(), calls=%async_computation.13 | async-start | bytes 2228224 | tf_op jit(solution)/shard_map/all_gather | solution.py:32
  588.9 5.9 collective-permute-start.3
  595.6 129.5 %reduce-scatter.14.cloned.1.call-start = ((), (), s32[]{:S(2)}) async-start(), calls=%async_computation.14 | async-start | bytes 2228224 | tf_op jit(solution)/shard_map/reduce_scatter | solution.py:59
  640.6 20.9 %copy-start.10 = (pred[128,128]{0,1:T(8,128)(4,1)S(1)}, pred[128,128]{0,1:T(8,128)(4,1)}, u32[]{:S(2)}) copy-start(pred[128,128]{0,1:T(8,128)(4,1)} %get-tuple-element.40) | copy-start | bytes 49156
  662.0 63.0 %copy-start.5 = (bf16[512,128]{0,1:T(8,128)(2,1)S(1)}, bf16[512,128]{0,1:T(8,128)(2,1)}, u32[]{:S(2)}) copy-start(bf16[512,128]{0,1:T(8,128)(2,1)} %get-tuple-element.8) | copy-start | bytes 393220
  666.4 8.7 %collective-permute-start.4 = (bf16[2,512,128]{1,2,0:T(8,128)(2,1)S(1)}, bf16[2,512,128]{1,2,0:T(8,128)(2,1)S(1)}, u32[]{:S(2)}, u32[]{:S(2)}) collective-permute-start(bf16[2,512,128]{1,2,0:T(8,128)(2,1)S(1)} %get-tuple-element.7), channel_id=1, source_target_pairs={{0,64},{64,0},{128,192},{192,128},{1,65},{65,1},{129,193},{193,129... | collective-permute-start | bytes 786440 | tf_op jit(solution)/shard_map/ppermute | solution.py:23
  675.0 9.3 %collective-permute-start.5 = (bf16[2,512,128]{1,2,0:T(8,128)(2,1)S(1)}, bf16[2,512,128]{1,2,0:T(8,128)(2,1)S(1)}, u32[]{:S(2)}, u32[]{:S(2)}) collective-permute-start(bf16[2,512,128]{1,2,0:T(8,128)(2,1)S(1)} %collective-permute-done.4), channel_id=1, source_target_pairs={{0,128},{64,192},{128,0},{192,64},{1,129},{65,193},{129,1},{193,65... | collective-permute-start | bytes 786440 | tf_op jit(solution)/shard_map/ppermute | solution.py:23
Sparse Core Ops, SparseCore 0:
  10.4 28.5 all-gather.8
  42.6 41.0 all-gather.18
  115.2 58.6 reduce-scatter.5
  181.7 39.1 all-gather.10
  253.1 58.4 reduce-scatter.7
  319.6 39.2 all-gather.12
  391.3 58.4 reduce-scatter.9
  457.5 39.3 all-gather.14
  529.2 58.6 reduce-scatter.11
  595.7 39.2 all-gather.16
  666.5 58.5 reduce-scatter.13
where the time goes:
time: 735 us; the launch traced here: 733 us
  waiting for transfers between devices  506 us (69%)
  blocking collectives  103 us (14%)
  matrix products  56.3 us (8%)
  other arithmetic  21.8 us (3%)
  starting transfers between devices  18.8 us (3%)
  between operations  14.5 us (2%)
  local copies, waits for them, and re-layouts  12.7 us (2%)
    reduce_scatter x5, waiting for transfers between devices, attention_layer(): lax.psum_scatter(lax.dot_general(out_weight, mixed, contract, preferred_e...  275 us
    all_gather x5, waiting for transfers between devices, attention_layer(): lax.all_gather(current, 'tp', axis=0, tiled=True)  179 us
    all_gather x5, blocking collectives, attention_layer(): lax.all_gather(keyvals.astype(jnp.bfloat16), 'tp', axis=1, tiled=True)  85.8 us
    all_gather x1, waiting for transfers between devices, shards(): gathered = lax.all_gather(rollout_acts, 'dp', axis=1, tiled=True)  28.4 us
    dot_general x5, matrix products, attention_layer(): lax.dot_general(out_weight, mixed, contract, preferred_element_type=jnp.f...  21.6 us
    dot_general x5, matrix products, attention_layer(): lax.dot_general(query_weight, normed, contract, preferred_element_type=jn...  17.9 us
    all_gather x1, blocking collectives, attention_layer(): lax.all_gather(gain_rows, 'tp', axis=0, tiled=True)  17.5 us
  transfers between devices with their start and end apart: 17, of which 17 were waited for; matrix products, arithmetic and copies ran while one was open for 1% of the time, Pallas kernels for 0%

commit v1 on v0

v1 whole, which is shorter than its diff:
```python
import functools

import jax
import jax.numpy as jnp
from jax import lax
from jax.experimental import pallas as pl
from jax.experimental.pallas import tpu as pltpu
from jax.sharding import Mesh
from jax.sharding import PartitionSpec as P

D = 8192
HD = 128
MICRO = 2
SEQ = 128
EPS = 1e-05
CHIPS = 8
SHARD = 512
HALF = SHARD // 2
STAT = 16
QROWS = 256
KVROWS = 256
ROWS = 2 * QROWS + KVROWS
ACC = ROWS + 8
ORDER = (0, -1, 1, -2, 2, -3, 3, 4)
BF = jnp.bfloat16
F32 = jnp.float32

GROUPS = 1


def z_shift(value, hops):
    return lax.ppermute(value, "z", [(i, (i + hops) % CHIPS) for i in range(CHIPS)])


def sibling(value):
    return lax.ppermute(value, "core", [(0, 1), (1, 0)])


def along_section(value, hops):
    count = lax.axis_size("section")
    return lax.ppermute(value, "section", [(i, (i + hops) % count) for i in range(count)])


def diagonal(value, hops):
    count = lax.axis_size("section")
    pairs = [
        (s * CHIPS + i, ((s + 1) % count) * CHIPS + (i + hops) % CHIPS)
        for s in range(count)
        for i in range(CHIPS)
    ]
    return lax.ppermute(value, ("section", "z"), pairs)


def kv_route(value, step):
    pairs = []
    for a in range(2):
        for b in range(4):
            for c in range(2):
                z = 4 * a + b
                pairs.append((2 * z + c, 2 * (a + 2 * ((b + 2 * c + step) % 4)) + b // 2))
    return lax.ppermute(value, ("z", "core"), pairs)


def full(shape):
    return pl.BlockSpec(shape, lambda i, idx: (0,) * len(shape))


def call(body, indices, operands, specs, outs, flops=0):
    nbytes = sum(o.size * o.dtype.itemsize for o in outs)
    return pl.pallas_call(
        body,
        grid_spec=pltpu.PrefetchScalarGridSpec(
            num_scalar_prefetch=1,
            grid=(1,),
            in_specs=specs,
            out_specs=[full(o.shape) for o in outs],
        ),
        out_shape=outs,
        compiler_params=pltpu.CompilerParams(vmem_limit_bytes=24 * 2**20),
        cost_estimate=pl.CostEstimate(flops=flops, bytes_accessed=nbytes, transcendentals=0),
    )(indices, *operands)


def prepare_body(idx, x_ref, gain_ref, out_ref):
    x = x_ref[...].astype(F32)
    tokens = x.shape[1]
    for col in range(0, tokens, SEQ):
        out_ref[0:SHARD, col : col + SEQ] = (x[:, col : col + SEQ] * gain_ref[...]).astype(BF)
    total = jnp.sum(x * x, axis=0, keepdims=True)
    high = total.astype(BF)
    low = (total - high.astype(F32)).astype(BF)
    rows = lax.broadcasted_iota(jnp.int32, (STAT, tokens), 0)
    stat = jnp.where(rows == 0, high.astype(F32), jnp.where(rows == 1, low.astype(F32), 0.0))
    out_ref[SHARD : SHARD + STAT, :] = stat.astype(BF)


def prepare(idx, x, gain):
    tokens = x.shape[1]
    (out,) = call(
        prepare_body,
        idx,
        (x, gain),
        [full(x.shape), full(gain.shape)],
        [jax.ShapeDtypeStruct((SHARD + STAT, tokens), BF)],
        flops=4 * x.size,
    )
    return out


def stat_of(block):
    return block[0:1, :].astype(F32) + block[1:2, :].astype(F32)


def project_body(count, halves, first, idx, *refs):
    refs = list(refs)
    (out_ref,) = refs[-1:]
    acc_ref = None if first else refs[0]
    refs = refs[0 if first else 1 : -1]
    chunks, weights = refs[: count + 2 * halves], refs[count + 2 * halves :]
    total = None if first else acc_ref[0:ROWS, :]
    stats = None if first else acc_ref[ROWS : ROWS + 1, :]
    for k in range(count):
        part = jnp.dot(weights[k][0], chunks[k][0:SHARD, :], preferred_element_type=F32)
        stat = stat_of(chunks[k][SHARD : SHARD + STAT, :])
        total = part if total is None else total + part
        stats = stat if stats is None else stats + stat
    if halves:
        low, high = chunks[count], chunks[count + 1]
        total = total + jnp.dot(
            weights[count][0, :, 0:HALF], low[0:HALF, :], preferred_element_type=F32
        )
        total = total + jnp.dot(
            weights[count][0, :, HALF:SHARD], high[0:HALF, :], preferred_element_type=F32
        )
        stats = stats + stat_of(high[HALF : HALF + STAT, :])
    out_ref[0:ROWS, :] = total
    out_ref[ROWS:ACC, :] = jnp.broadcast_to(stats, (8, stats.shape[1]))


def project(idx, acc, chunks, places, weights, halves=()):
    tokens = chunks[0].shape[1]
    count = len(chunks)
    arrays = list(chunks) + list(halves)
    operands = ([] if acc is None else [acc]) + arrays
    specs = [full(a.shape) for a in operands]
    for place in places:
        specs.append(
            pl.BlockSpec((1, ROWS, SHARD), lambda i, idx, place=place: (idx[place], 0, 0))
        )
        operands.append(weights)
    (out,) = call(
        functools.partial(project_body, count, len(halves) // 2, acc is None),
        idx,
        operands,
        specs,
        [jax.ShapeDtypeStruct((ACC, tokens), F32)],
        flops=2 * ROWS * SHARD * tokens * len(places),
    )
    return out


def finish_body(idx, acc_ref, recv_ref, q_ref, kv_ref):
    total = acc_ref[ROWS : ROWS + 1, :] + recv_ref[512:513, :]
    scale = lax.rsqrt(total * (1.0 / D) + EPS)
    q_ref[...] = ((acc_ref[0:256, :] + recv_ref[256:512, :]) * scale).astype(BF)
    kv_ref[...] = ((acc_ref[256:512, :] + recv_ref[0:256, :]) * scale).astype(BF)


def finish(idx, acc, recv):
    tokens = acc.shape[1]
    return call(
        finish_body,
        idx,
        (acc, recv),
        [full(acc.shape), full(recv.shape)],
        [
            jax.ShapeDtypeStruct((QROWS, tokens), BF),
            jax.ShapeDtypeStruct((KVROWS, tokens), BF),
        ],
        flops=4 * 512 * tokens,
    )


def attend_body(idx, q_ref, first_ref, second_ref, mask_ref, out_ref):
    flip = idx[CHIPS] == 1
    tokens = q_ref.shape[1]
    for row in range(tokens // SEQ):
        cols = slice(row * SEQ, (row + 1) * SEQ)
        allowed = mask_ref[row] > 0.0
        one, two = first_ref[:, cols], second_ref[:, cols]
        for head in range(2):
            pair = jnp.where(flip, two, one) if head == 0 else jnp.where(flip, one, two)
            q = q_ref[head * HD : (head + 1) * HD, cols]
            scores = lax.dot_general(
                pair[0:HD, :], q, (((0,), (0,)), ((), ())), preferred_element_type=F32
            ) * HD ** (-0.5)
            weights = jnp.where(allowed, jnp.exp(jnp.where(allowed, scores, 0.0)), 0.0)
            probs = (weights / jnp.sum(weights, axis=0, keepdims=True)).astype(BF)
            mixed = jnp.dot(pair[HD : 2 * HD, :], probs, preferred_element_type=F32)
            out_ref[head * HD : (head + 1) * HD, cols] = mixed.astype(BF)


def attend(idx, q, first, second, mask):
    (out,) = call(
        attend_body,
        idx,
        (q, first, second, mask),
        [full(a.shape) for a in (q, first, second, mask)],
        [jax.ShapeDtypeStruct(q.shape, BF)],
        flops=8 * HD * SEQ * q.shape[1],
    )
    return out


def spread_body(kinds, idx, own_ref, other_ref, *refs):
    count = len(kinds)
    weights, outs = refs[:count], refs[count:]
    flip = idx[CHIPS + 1] == 1
    own, other = own_ref[...], other_ref[...]
    heads = jnp.concatenate(
        [jnp.where(flip, other, own), jnp.where(flip, own, other)], axis=0
    )
    for k in range(count):
        part = jnp.dot(weights[k][0], heads, preferred_element_type=F32)
        outs[k][...] = part.astype(outs[k].dtype)


def spread(idx, own, other, places, kinds, weights):
    tokens = own.shape[1]
    specs = [full(own.shape), full(other.shape)]
    operands = [own, other]
    for place in places:
        specs.append(
            pl.BlockSpec((1, SHARD, SHARD), lambda i, idx, place=place: (idx[place], 0, 0))
        )
        operands.append(weights)
    return call(
        functools.partial(spread_body, kinds),
        idx,
        operands,
        specs,
        [jax.ShapeDtypeStruct((SHARD, tokens), kind) for kind in kinds],
        flops=2 * SHARD * SHARD * tokens * len(places),
    )


def gather_project(idx, payload, w_in):
    right1, left1 = z_shift(payload, 1), z_shift(payload, -1)
    acc = project(idx, None, [payload], [0], w_in)
    right2, left2 = z_shift(right1, 1), z_shift(left1, -1)
    acc = project(idx, acc, [right1, left1], [1, 2], w_in)
    right3, left3 = z_shift(right2, 1), z_shift(left2, -1)
    right4, left4 = z_shift(right2[:HALF], 2), z_shift(left2[HALF:], -2)
    acc = project(idx, acc, [right2, left2], [3, 4], w_in)
    return project(idx, acc, [right3, left3], [5, 6, 7], w_in, (right4, left4))


def layer(idx, x, payload, mask, w_in, w_out, last):
    acc = gather_project(idx, payload, w_in)
    recv = sibling(acc[QROWS:])
    q, kv = finish(idx, acc, recv)
    first, second = kv_route(kv, 0), kv_route(kv, 1)
    mixed = attend(idx, q, first, second, mask)
    other = sibling(mixed)
    far_left, far_right, opposite = spread(idx, mixed, other, [5, 6, 7], (BF,) * 3, w_out)
    to_right, to_left = z_shift(far_right, 1), z_shift(far_left, -1)
    low, high = z_shift(opposite[:HALF], 2), z_shift(opposite[HALF:], -2)
    two_left, two_right, one_left, one_right, own = spread(
        idx, mixed, other, [3, 4, 1, 2, 0], (F32,) * 5, w_out
    )
    base = x.astype(F32) + own
    zeros = jnp.zeros_like(low)
    to_right = (
        two_right + to_right.astype(F32) + jnp.concatenate([low, zeros], 0).astype(F32)
    ).astype(BF)
    to_left = (
        two_left + to_left.astype(F32) + jnp.concatenate([zeros, high], 0).astype(F32)
    ).astype(BF)
    if not last:
        base = along_section(base.astype(BF), 1).astype(F32)
    to_right, to_left = z_shift(to_right, 1), z_shift(to_left, -1)
    to_right = (one_right + to_right.astype(F32)).astype(BF)
    to_left = (one_left + to_left.astype(F32)).astype(BF)
    move = z_shift if last else diagonal
    to_right, to_left = move(to_right, 1), move(to_left, -1)
    return (base + to_right.astype(F32) + to_left.astype(F32)).astype(BF)


def pack(rollout, source):
    tokens = rollout.shape[1]
    place = lax.axis_index("dp")
    count = lax.axis_size("dp")
    blocks = [rollout]
    for hops in range(1, count):
        pairs = [(i, (i + hops) % count) for i in range(count)]
        blocks.append(lax.ppermute(rollout, "dp", pairs))
    ids = jnp.concatenate(
        [
            (place - hops) % count * tokens + jnp.arange(tokens, dtype=jnp.int32)
            for hops in range(count)
        ]
    )
    chosen = (ids[:, None] == source[None, :]).astype(BF)
    return jnp.dot(
        jnp.concatenate(blocks, axis=1), chosen, preferred_element_type=F32
    ).astype(BF)


def weights_in(wq, wkv, core):
    q_all = wq.reshape(CHIPS, 2, SHARD, QROWS)
    kv_all = wkv.reshape(2, CHIPS, 2, SHARD, HD // 2)
    pick_q = lambda c: lax.dynamic_index_in_dim(q_all, c, 1, keepdims=False).transpose(0, 2, 1)
    pick_kv = lambda c: lax.dynamic_index_in_dim(kv_all, c, 2, keepdims=False).transpose(1, 0, 3, 2)
    q_own, kv_own = pick_q(core), pick_kv(core)
    q_other, kv_other = sibling(pick_q(1 - core)), sibling(pick_kv(1 - core))
    pair = jnp.where(
        core == 0,
        jnp.stack([kv_own, kv_other], axis=2),
        jnp.stack([kv_other, kv_own], axis=2),
    )
    return jnp.concatenate([q_own, pair.reshape(CHIPS, KVROWS, SHARD), q_other], axis=1)


def weights_out(wo, core):
    all_out = wo.reshape(QROWS, CHIPS, 2, SHARD)
    pick = lambda c: lax.dynamic_index_in_dim(all_out, c, 2, keepdims=False).transpose(1, 2, 0)
    own, other = pick(core), sibling(pick(1 - core))
    return jnp.where(
        core == 0, jnp.concatenate([own, other], 2), jnp.concatenate([other, own], 2)
    )


def shards(rollout_acts, pack_source, segments, gain, wq, wkv, wo):
    section = lax.axis_index("section")
    count = lax.axis_size("section")
    z, core = lax.axis_index("z"), lax.axis_index("core")
    idx = jnp.stack([(z + k) % CHIPS for k in ORDER] + [(z // 2) % 2, core]).astype(jnp.int32)
    x = pack(rollout_acts, pack_source[0].reshape(-1))
    w_in = weights_in(wq[0], wkv[0], core)
    w_out = weights_out(wo[0], core)
    gains = jnp.broadcast_to(gain[0].astype(F32)[:, None], (SHARD, SEQ))
    seg = segments[0]
    spots = jnp.arange(SEQ, dtype=jnp.int32)
    mask = (
        (seg[:, :, None] == seg[:, None, :]) & (spots[:, None] <= spots[None, :])[None]
    ).astype(F32)
    taken = x
    for step in range(count):
        taken = jnp.where(section == step, x, taken)
        last = step == count - 1
        if last:
            mirrored = lax.ppermute(
                taken, "section", [(i, count - 1 - i) for i in range(count)]
            )
            produced = along_section(taken, -1)
        payload = prepare(idx, x, gains)
        x = layer(idx, x, payload, mask, w_in, w_out, last)
    produced = jnp.where(section == count - 1, x, produced)
    arrange = lambda v: v.reshape(SHARD, MICRO, SEQ).transpose(1, 0, 2)[None, None]
    return (arrange(produced), arrange(mirrored))


def solution(mesh):
    devices = mesh.devices
    sections, ways, replicas = devices.shape
    fine = Mesh(devices.reshape(sections, ways // 2, 2, replicas), ("section", "z", "core", "dp"))
    tp = ("z", "core")
    in_specs = (
        P(tp, "dp"),
        P("dp", None, None),
        P("dp", None, None),
        P("section", tp),
        P("section", None, tp),
        P("section", None, None, tp),
        P("section", tp, None),
    )
    out_specs = (P("section", "dp", None, tp, None), P("section", "dp", None, tp, None))
    return jax.shard_map(shards, mesh=fine, in_specs=in_specs, out_specs=out_specs, check_vma=False)
```

time: 735 us -> 453 us (0.62)
  waiting for transfers between devices: 506 us -> 162 us
  starting transfers between devices: 18.8 us -> 161 us
  blocking collectives: 103 us -> 0 us
  local copies, waits for them, and re-layouts: 12.7 us -> 70.4 us
  matrix products: 56.3 us -> 0.56 us
  Pallas kernels: 0 us -> 36.7 us
  between operations: 14.5 us -> 2.08 us
  other arithmetic: 21.8 us -> 12.3 us
    reduce_scatter x5 -> x0, waiting for transfers between devices: 275 us -> none  [attention_layer(): lax.psum_scatter(lax.dot_general(out_weight, mixed, contract, preferred_e...]
    all_gather x6 -> x0, waiting for transfers between devices: 208 us -> none  [the longest x5 179 us: attention_layer(): lax.all_gather(current, 'tp', axis=0, tiled=True)]
    ppermute x6 -> x91, starting transfers between devices: 18.3 us -> 161 us  [the longest x58 104 us: z_shift(): lax.ppermute(value, 'z', [(i, (i + hops) % CHIPS) for i in range(CHIPS)])]
    ppermute x6 -> x91, waiting for transfers between devices: 23.3 us -> 162 us  [the longest x58 104 us: z_shift(): lax.ppermute(value, 'z', [(i, (i + hops) % CHIPS) for i in range(CHIPS)])]
    all_gather x6 -> x0, blocking collectives: 103 us -> none  [the longest x5 85.8 us: attention_layer(): lax.all_gather(keyvals.astype(jnp.bfloat16), 'tp', axis=1, tiled=True)]
    dot_general x20 -> x1, matrix products: 44.2 us -> 0.56 us  [pack(): jnp.dot(jnp.concatenate(blocks, axis=1), chosen, preferred_element_type=F32)]
    pallas_call x0 -> x36, Pallas kernels: none -> 36.7 us  [call(): pl.pallas_call(body, grid_spec=pltpu.PrefetchScalarGridSpec(num_scalar_pr...]
    dynamic_slice x0 -> x5, local copies, waits for them, and re-layouts: none -> 27.9 us  [the longest x1 13.4 us: weights_out(): lax.dynamic_index_in_dim(all_out, c, 2, keepdims=False).transpose(1, 2, 0)]
  transfers between devices with their start and end apart: 17 -> 91, of which waited for: 17 -> 44; matrix products, arithmetic and copies ran while one was open for 1% -> 18% of each run, Pallas kernels for 0% -> 5%
where the time goes in v1:
time: 453 us; the launch traced here: 445 us
  waiting for transfers between devices  162 us (36%)
  starting transfers between devices  161 us (36%)
  local copies, waits for them, and re-layouts  70.4 us (16%)
  Pallas kernels  36.7 us (8%)
  other arithmetic  12.3 us (3%)
    ppermute x58, starting transfers between devices, z_shift(): lax.ppermute(value, 'z', [(i, (i + hops) % CHIPS) for i in range(CHIPS)])  104 us
    ppermute x58, waiting for transfers between devices, z_shift(): lax.ppermute(value, 'z', [(i, (i + hops) % CHIPS) for i in range(CHIPS)])  104 us
    pallas_call x36, Pallas kernels, call(): pl.pallas_call(body, grid_spec=pltpu.PrefetchScalarGridSpec(num_scalar_pr...  36.7 us
    ppermute x4, waiting for transfers between devices, along_section(): lax.ppermute(value, 'section', [(i, (i + hops) % count) for i in range(co...  34.1 us
    unnamed x28, local copies, waits for them, and re-layouts  30.2 us
    ppermute x11, starting transfers between devices, sibling(): return lax.ppermute(value, 'core', [(0, 1), (1, 0)])  22.5 us
    ppermute x8, waiting for transfers between devices, kv_route(): return lax.ppermute(value, ('z', 'core'), pairs)  15.3 us
    dynamic_slice x1, local copies, waits for them, and re-layouts, weights_out(): lax.dynamic_index_in_dim(all_out, c, 2, keepdims=False).transpose(1, 2, 0)  13.4 us
  transfers between devices with their start and end apart: 91, of which 44 were waited for; matrix products, arithmetic and copies ran while one was open for 18% of the time, Pallas kernels for 5%

profile of v1, /device:TPU:2, one launch (start us, length us, event | category | flops | bytes accessed | tf_op | source)
XLA Modules:
  0.0 444.8 jit_solution(1101094775829314435)
XLA Ops:
  4.9 3.9 constant_dynamic-slice_fusion.5
  11.1 3.3 reshape_squeeze.10
  14.4 5.8 %constant_dynamic-slice_fusion.4 = (bf16[2,8,1,512,64]{3,2,1,4,0:T(2,128)(2,1)}, bf16[2,8,1,512,64]{3,2,1,4,0:T(2,128)(2,1)S(1)}) fusion(bf16[2,8,2,512,64]{3,2,1,4,0:T(2,128)(2,1)S(1)} %reshape_squeeze.10, s32[]{:T(128)S(6)} %select_n.133, s32[]{:T(128)S(6)} %select_n.135), kind=kLoop, calls=%fused_computation.51 | loop fusion | bytes 4194312 | tf_op jit(solution)/shard_map/jit(dynamic_index_in_dim)/dynamic_slice | solution.py:313
  23.0 7.8 %reshape_squeeze.11 = bf16[256,8,2,512]{3,2,1,0:T(2,128)(2,1)} reshape(bf16[1,256,8192]{2,1,0:T(8,128)(2,1)} %param.13) | data formatting | bytes 8388608 | tf_op jit(solution)/shard_map/reshape;squeeze | solution.py:325
  30.9 13.4 %constant_dynamic-slice_fusion.1 = (bf16[256,8,1,512]{3,2,1,0:T(2,128)(2,1)}, bf16[256,8,1,512]{3,2,1,0:T(2,128)(2,1)}) fusion(bf16[256,8,2,512]{3,2,1,0:T(2,128)(2,1)} %reshape_squeeze.11, s32[]{:T(128)S(6)} %select_n.133, s32[]{:T(128)S(6)} %select_n.135), kind=kLoop, calls=%fused_computation.48 | loop fusion | bytes 8388616 | tf_op jit(solution)/shard_map/jit(dynamic_index_in_dim)/dynamic_slice | solution.py:326
  44.5 10.5 %copy.20 = bf16[256,8,1,512]{0,3,1,2:T(8,128)(2,1)} copy(bf16[256,8,1,512]{3,2,1,0:T(2,128)(2,1)} %get-tuple-element.85) | data formatting | bytes 4194304
  56.6 5.9 %collective-permute-start.6 = (bf16[528,256]{1,0:T(8,128)(2,1)S(1)}, bf16[528,256]{1,0:T(8,128)(2,1)S(1)}, u32[]{:S(2)}, u32[]{:S(2)}) collective-permute-start(bf16[528,256]{1,0:T(8,128)(2,1)S(1)} %shard_map.86.refs_0_), channel_id=1, source_target_pairs={{0,56},{8,0},{16,8},{24,16},{32,24},{40,32},{48,40},{56,48},{1,57}... | collective-permute-start | bytes 811016 | tf_op jit(solution)/shard_map/ppermute | solution.py:32
  62.6 6.4 %collective-permute-done.6.refs_2_ = bf16[528,256]{1,0:T(8,128)(2,1)S(1)} collective-permute-done((bf16[528,256]{1,0:T(8,128)(2,1)S(1)}, bf16[528,256]{1,0:T(8,128)(2,1)S(1)}, u32[]{:S(2)}, u32[]{:S(2)}) %collective-permute-start.6) | collective-permute-done | bytes 270368 | tf_op jit(solution)/shard_map/ppermute | solution.py:32
  68.9 3.7 collective-permute-start.8
  72.6 2.7 copy.28
  75.3 3.9 copy.17
  82.4 4.4 collective-permute-start.10
  89.3 4.6 %pad_maximum_fusion.refs_1_.refs_3_.refs_4_.refs_5_.refs_6_.refs_7_ = bf16[8,768,512]{2,1,0:T(8,128)(2,1)S(1)} fusion(bf16[8,256,512]{2,1,0:T(8,128)(2,1)} %collective-permute-done.4, bf16[8,256,512]{2,1,0:T(8,128)(2,1)S(1)} %bitcast.66, bf16[8,256,512]{2,1,0:T(8,128)(2,1)S(1)} %bitcast.65), kind=kLoop, calls=%fused_computation | loop fusion | flops 18874368 | bytes 12582912 | tf_op jit(solution)/shard_map/concatenate | solution.py:321
  98.7 10.5 %copy.19 = bf16[256,8,1,512]{0,3,1,2:T(8,128)(2,1)} copy(bf16[256,8,1,512]{3,2,1,0:T(2,128)(2,1)} %get-tuple-element.84) | data formatting | bytes 4194304
  112.5 3.6 collective-permute-done.15.second_ref
  117.0 5.8 %collective-permute-start.16 = (bf16[256,256]{1,0:T(8,128)(2,1)S(1)}, bf16[256,256]{1,0:T(8,128)(2,1)S(1)}, u32[]{:S(2)}, u32[]{:S(2)}) collective-permute-start(bf16[256,256]{1,0:T(8,128)(2,1)S(1)} %shard_map.92.own_ref), channel_id=1, source_target_pairs={{0,4},{4,0},{1,5},{5,1},{2,6},{6,2},{3,7},{7,3},{8,12},{12,8},{9,1... | collective-permute-start | bytes 393224 | tf_op jit(solution)/shard_map/ppermute | solution.py:36
  122.9 3.2 maximum_select_fusion.refs_0_.refs_1_.refs_2_.refs_3_.refs_4_
  127.2 5.2 %collective-permute-start.19 = (bf16[512,256]{1,0:T(8,128)(2,1)S(1)}, bf16[512,256]{1,0:T(8,128)(2,1)S(1)}, u32[]{:S(2)}, u32[]{:S(2)}) collective-permute-start(bf16[512,256]{1,0:T(8,128)(2,1)S(1)} %get-tuple-element.47), channel_id=1, source_target_pairs={{0,8},{8,16},{16,24},{24,32},{32,40},{40,48},{48,56},{56,0},{1,9},... | collective-permute-start | bytes 786440 | tf_op jit(solution)/shard_map/ppermute | solution.py:32
  132.6 4.1 collective-permute-start.24
  138.1 6.2 %collective-permute-done.20 = bf16[256,256]{1,0:T(8,128)(2,1)S(1)} collective-permute-done((bf16[256,256]{1,0:T(8,128)(2,1)S(1)}, bf16[256,256]{1,0:T(8,128)(2,1)S(1)}, u32[]{:S(2)}, u32[]{:S(2)}) %collective-permute-start.20) | collective-permute-done | bytes 131104 | tf_op jit(solution)/shard_map/ppermute | solution.py:32
  144.5 3.4 collective-permute-done.23
  148.0 3.8 collective-permute-start.25
  157.2 4.8 %collective-permute-start.26 = (bf16[512,256]{1,0:T(8,128)(2,1)S(1)}, bf16[512,256]{1,0:T(8,128)(2,1)S(1)}, u32[]{:S(2)}, u32[]{:S(2)}) collective-permute-start(bf16[512,256]{1,0:T(8,128)(2,1)S(1)} %add_convert_fusion.18), channel_id=1, source_target_pairs={{0,120},{8,64},{16,72},{24,80},{32,88},{40,96},{48,104},{56,112},{... | collective-permute-start | bytes 786440 | tf_op jit(solution)/shard_map/ppermute | solution.py:51
  161.9 10.0 %collective-permute-done.18 = bf16[512,256]{1,0:T(8,128)(2,1)S(1)} collective-permute-done((bf16[512,256]{1,0:T(8,128)(2,1)S(1)}, bf16[512,256]{1,0:T(8,128)(2,1)S(1)}, u32[]{:S(2)}, u32[]{:S(2)}) %collective-permute-start.18) | collective-permute-done | bytes 262176 | tf_op jit(solution)/shard_map/ppermute | solution.py:41
  174.8 4.8 %collective-permute-done.28.refs_2_ = bf16[528,256]{1,0:T(8,128)(2,1)S(1)} collective-permute-done((bf16[528,256]{1,0:T(8,128)(2,1)S(1)}, bf16[528,256]{1,0:T(8,128)(2,1)S(1)}, u32[]{:S(2)}, u32[]{:S(2)}) %collective-permute-start.28) | collective-permute-done | bytes 270368 | tf_op jit(solution)/shard_map/ppermute | solution.py:32
  181.7 5.4 %collective-permute-done.30.refs_2_ = bf16[528,256]{1,0:T(8,128)(2,1)S(1)} collective-permute-done((bf16[528,256]{1,0:T(8,128)(2,1)S(1)}, bf16[528,256]{1,0:T(8,128)(2,1)S(1)}, u32[]{:S(2)}, u32[]{:S(2)}) %collective-permute-start.30) | collective-permute-done | bytes 270368 | tf_op jit(solution)/shard_map/ppermute | solution.py:32
  195.3 3.5 collective-permute-done.33.refs_3_
  205.9 4.3 collective-permute-done.37.second_ref
  211.2 4.8 %collective-permute-start.38 = (bf16[256,256]{1,0:T(8,128)(2,1)S(1)}, bf16[256,256]{1,0:T(8,128)(2,1)S(1)}, u32[]{:S(2)}, u32[]{:S(2)}) collective-permute-start(bf16[256,256]{1,0:T(8,128)(2,1)S(1)} %shard_map.101.own_ref), channel_id=1, source_target_pairs={{0,4},{4,0},{1,5},{5,1},{2,6},{6,2},{3,7},{7,3},{8,12},{12,8},{9,1... | collective-permute-start | bytes 393224 | tf_op jit(solution)/shard_map/ppermute | solution.py:36
  218.1 5.6 %collective-permute-start.40 = (bf16[512,256]{1,0:T(8,128)(2,1)S(1)}, bf16[512,256]{1,0:T(8,128)(2,1)S(1)}, u32[]{:S(2)}, u32[]{:S(2)}) collective-permute-start(bf16[512,256]{1,0:T(8,128)(2,1)S(1)} %get-tuple-element.57), channel_id=1, source_target_pairs={{0,8},{8,16},{16,24},{24,32},{32,40},{40,48},{48,56},{56,0},{1,9},... | collective-permute-start | bytes 786440 | tf_op jit(solution)/shard_map/ppermute | solution.py:32
  224.2 4.1 collective-permute-start.45
  229.7 5.5 %collective-permute-done.41 = bf16[256,256]{1,0:T(8,128)(2,1)S(1)} collective-permute-done((bf16[256,256]{1,0:T(8,128)(2,1)S(1)}, bf16[256,256]{1,0:T(8,128)(2,1)S(1)}, u32[]{:S(2)}, u32[]{:S(2)}) %collective-permute-start.41) | collective-permute-done | bytes 131104 | tf_op jit(solution)/shard_map/ppermute | solution.py:32
  235.8 3.4 collective-permute-done.44
  239.3 3.8 collective-permute-start.46
  245.3 3.4 collective-permute-done.46
  248.7 3.7 collective-permute-start.47
  252.4 11.1 %collective-permute-done.39 = bf16[512,256]{1,0:T(8,128)(2,1)S(1)} collective-permute-done((bf16[512,256]{1,0:T(8,128)(2,1)S(1)}, bf16[512,256]{1,0:T(8,128)(2,1)S(1)}, u32[]{:S(2)}, u32[]{:S(2)}) %collective-permute-start.39) | collective-permute-done | bytes 262176 | tf_op jit(solution)/shard_map/ppermute | solution.py:41
  266.3 5.0 %collective-permute-done.49.refs_2_ = bf16[528,256]{1,0:T(8,128)(2,1)S(1)} collective-permute-done((bf16[528,256]{1,0:T(8,128)(2,1)S(1)}, bf16[528,256]{1,0:T(8,128)(2,1)S(1)}, u32[]{:S(2)}, u32[]{:S(2)}) %collective-permute-start.49) | collective-permute-done | bytes 270368 | tf_op jit(solution)/shard_map/ppermute | solution.py:32
  273.4 5.2 %collective-permute-done.51.refs_2_ = bf16[528,256]{1,0:T(8,128)(2,1)S(1)} collective-permute-done((bf16[528,256]{1,0:T(8,128)(2,1)S(1)}, bf16[528,256]{1,0:T(8,128)(2,1)S(1)}, u32[]{:S(2)}, u32[]{:S(2)}) %collective-permute-start.51) | collective-permute-done | bytes 270368 | tf_op jit(solution)/shard_map/ppermute | solution.py:32
  280.6 4.5 %collective-permute-start.55 = (bf16[272,256]{1,0:T(8,128)(2,1)S(1)}, bf16[272,256]{1,0:T(8,128)(2,1)S(1)}, u32[]{:S(2)}, u32[]{:S(2)}) collective-permute-start(bf16[272,256]{1,0:T(8,128)(2,1)S(1)} %slice.87), channel_id=1, source_target_pairs={{0,48},{8,56},{16,0},{24,8},{32,16},{40,24},{48,32},{56,40},{1,49}... | collective-permute-start | bytes 417800 | tf_op jit(solution)/shard_map/ppermute | solution.py:32
  288.6 5.4 %collective-permute-done.54.refs_3_ = bf16[256,256]{1,0:T(8,128)(2,1)S(1)} collective-permute-done((bf16[256,256]{1,0:T(8,128)(2,1)S(1)}, bf16[256,256]{1,0:T(8,128)(2,1)S(1)}, u32[]{:S(2)}, u32[]{:S(2)}) %collective-permute-start.54) | collective-permute-done | bytes 131104 | tf_op jit(solution)/shard_map/ppermute | solution.py:32
  300.6 3.7 collective-permute-done.58.second_ref
  305.2 4.4 collective-permute-start.59
  311.8 4.9 %collective-permute-start.61 = (bf16[512,256]{1,0:T(8,128)(2,1)S(1)}, bf16[512,256]{1,0:T(8,128)(2,1)S(1)}, u32[]{:S(2)}, u32[]{:S(2)}) collective-permute-start(bf16[512,256]{1,0:T(8,128)(2,1)S(1)} %get-tuple-element.67), channel_id=1, source_target_pairs={{0,8},{8,16},{16,24},{24,32},{32,40},{40,48},{48,56},{56,0},{1,9},... | collective-permute-start | bytes 786440 | tf_op jit(solution)/shard_map/ppermute | solution.py:32
  316.7 4.1 collective-permute-start.66
  322.3 5.9 %collective-permute-done.62 = bf16[256,256]{1,0:T(8,128)(2,1)S(1)} collective-permute-done((bf16[256,256]{1,0:T(8,128)(2,1)S(1)}, bf16[256,256]{1,0:T(8,128)(2,1)S(1)}, u32[]{:S(2)}, u32[]{:S(2)}) %collective-permute-start.62) | collective-permute-done | bytes 131104 | tf_op jit(solution)/shard_map/ppermute | solution.py:32
  329.0 3.1 collective-permute-done.65
  332.1 3.2 collective-permute-start.67
  337.3 2.7 collective-permute-done.67
  340.1 2.7 collective-permute-start.68
  342.8 12.0 %collective-permute-done.60 = bf16[512,256]{1,0:T(8,128)(2,1)S(1)} collective-permute-done((bf16[512,256]{1,0:T(8,128)(2,1)S(1)}, bf16[512,256]{1,0:T(8,128)(2,1)S(1)}, u32[]{:S(2)}, u32[]{:S(2)}) %collective-permute-start.60) | collective-permute-done | bytes 262176 | tf_op jit(solution)/shard_map/ppermute | solution.py:41
  358.0 6.1 %collective-permute-done.70.refs_2_ = bf16[528,256]{1,0:T(8,128)(2,1)S(1)} collective-permute-done((bf16[528,256]{1,0:T(8,128)(2,1)S(1)}, bf16[528,256]{1,0:T(8,128)(2,1)S(1)}, u32[]{:S(2)}, u32[]{:S(2)}) %collective-permute-start.70) | collective-permute-done | bytes 270368 | tf_op jit(solution)/shard_map/ppermute | solution.py:32
  366.2 7.2 %collective-permute-done.72.refs_2_ = bf16[528,256]{1,0:T(8,128)(2,1)S(1)} collective-permute-done((bf16[528,256]{1,0:T(8,128)(2,1)S(1)}, bf16[528,256]{1,0:T(8,128)(2,1)S(1)}, u32[]{:S(2)}, u32[]{:S(2)}) %collective-permute-start.72) | collective-permute-done | bytes 270368 | tf_op jit(solution)/shard_map/ppermute | solution.py:32
  378.7 2.8 copy-done.1
  388.7 2.7 collective-permute-start.79
  392.0 3.8 collective-permute-done.79.second_ref
  396.8 6.2 %collective-permute-start.80 = (bf16[256,256]{1,0:T(8,128)(2,1)S(1)}, bf16[256,256]{1,0:T(8,128)(2,1)S(1)}, u32[]{:S(2)}, u32[]{:S(2)}) collective-permute-start(bf16[256,256]{1,0:T(8,128)(2,1)S(1)} %shard_map.119.own_ref), channel_id=1, source_target_pairs={{0,4},{4,0},{1,5},{5,1},{2,6},{6,2},{3,7},{7,3},{8,12},{12,8},{9,1... | collective-permute-start | bytes 393224 | tf_op jit(solution)/shard_map/ppermute | solution.py:36
  405.1 6.1 %collective-permute-start.81 = (bf16[512,256]{1,0:T(8,128)(2,1)S(1)}, bf16[512,256]{1,0:T(8,128)(2,1)S(1)}, u32[]{:S(2)}, u32[]{:S(2)}) collective-permute-start(bf16[512,256]{1,0:T(8,128)(2,1)S(1)} %get-tuple-element.77), channel_id=1, source_target_pairs={{0,8},{8,16},{16,24},{24,32},{32,40},{40,48},{48,56},{56,0},{1,9},... | collective-permute-start | bytes 786440 | tf_op jit(solution)/shard_map/ppermute | solution.py:32
  411.4 4.1 collective-permute-start.86
  417.1 5.6 %collective-permute-done.82 = bf16[256,256]{1,0:T(8,128)(2,1)S(1)} collective-permute-done((bf16[256,256]{1,0:T(8,128)(2,1)S(1)}, bf16[256,256]{1,0:T(8,128)(2,1)S(1)}, u32[]{:S(2)}, u32[]{:S(2)}) %collective-permute-start.82) | collective-permute-done | bytes 131104 | tf_op jit(solution)/shard_map/ppermute | solution.py:32
  423.4 3.0 collective-permute-done.85
  426.4 3.8 collective-permute-start.87
  430.2 3.2 collective-permute-start.89
  435.5 3.8 collective-permute-start.88
  (242 shorter events, 117.4 us)
Async XLA Ops:
  0.6 54.5 %collective-permute-start.1 = (bf16[512,256]{1,0:T(8,128)(2,1)}, bf16[512,256]{1,0:T(8,128)(2,1)S(1)}, u32[]{:S(2)}, u32[]{:S(2)}) collective-permute-start(bf16[512,256]{1,0:T(8,128)(2,1)} %param.7), channel_id=1, source_target_pairs={{0,2},{1,3},{2,0},{3,1},{4,6},{5,7},{6,4},{7,5},{8,10},{9,11},{10,... | collective-permute-start | bytes 786440 | tf_op jit(solution)/shard_map/ppermute | solution.py:296
  2.8 52.4 %collective-permute-start = (bf16[512,256]{1,0:T(8,128)(2,1)}, bf16[512,256]{1,0:T(8,128)(2,1)S(1)}, u32[]{:S(2)}, u32[]{:S(2)}) collective-permute-start(bf16[512,256]{1,0:T(8,128)(2,1)} %param.7), channel_id=1, source_target_pairs={{0,1},{1,2},{2,3},{3,0},{4,5},{5,6},{6,7},{7,4},{8,9},{9,10},{10,1... | collective-permute-start | bytes 786440 | tf_op jit(solution)/shard_map/ppermute | solution.py:296
  4.5 50.8 %collective-permute-start.2 = (bf16[512,256]{1,0:T(8,128)(2,1)}, bf16[512,256]{1,0:T(8,128)(2,1)S(1)}, u32[]{:S(2)}, u32[]{:S(2)}) collective-permute-start(bf16[512,256]{1,0:T(8,128)(2,1)} %param.7), channel_id=1, source_target_pairs={{0,3},{1,0},{2,1},{3,2},{4,7},{5,4},{6,5},{7,6},{8,11},{9,8},{10,9... | collective-permute-start | bytes 786440 | tf_op jit(solution)/shard_map/ppermute | solution.py:296
  11.1 77.7 %collective-permute-start.4 = (bf16[8,256,512]{2,1,0:T(8,128)(2,1)}, bf16[8,256,512]{2,1,0:T(8,128)(2,1)}, u32[]{:S(2)}, u32[]{:S(2)}) collective-permute-start(bf16[8,256,512]{2,1,0:T(8,128)(2,1)} %bitcast.69), channel_id=1, source_target_pairs={{0,4},{4,0},{1,5},{5,1},{2,6},{6,2},{3,7},{7,3},{8,12},{12,8},{9,1... | collective-permute-start | bytes 6291464 | tf_op jit(solution)/shard_map/ppermute | solution.py:36
  22.3 60.1 %collective-permute-start.3 = (bf16[8,2,64,512]{3,2,1,0:T(8,128)(2,1)}, bf16[8,2,64,512]{3,2,1,0:T(8,128)(2,1)}, u32[]{:S(2)}, u32[]{:S(2)}) collective-permute-start(bf16[8,2,64,512]{3,2,1,0:T(8,128)(2,1)} %bitcast.60), channel_id=1, source_target_pairs={{0,4},{4,0},{1,5},{5,1},{2,6},{6,2},{3,7},{7,3},{8,12},{12,8},{9,1... | collective-permute-start | bytes 3145736 | tf_op jit(solution)/shard_map/ppermute | solution.py:36
  55.1 67.8 %collective-permute-start.17 = (bf16[8,512,256]{2,1,0:T(8,128)(2,1)}, bf16[8,512,256]{2,1,0:T(8,128)(2,1)}, u32[]{:S(2)}, u32[]{:S(2)}) collective-permute-start(bf16[8,512,256]{2,1,0:T(8,128)(2,1)} %bitcast.30), channel_id=1, source_target_pairs={{0,4},{4,0},{1,5},{5,1},{2,6},{6,2},{3,7},{7,3},{8,12},{12,8},{9,1... | collective-permute-start | bytes 6291464 | tf_op jit(solution)/shard_map/ppermute | solution.py:36
  56.6 12.3 %collective-permute-start.6 = (bf16[528,256]{1,0:T(8,128)(2,1)S(1)}, bf16[528,256]{1,0:T(8,128)(2,1)S(1)}, u32[]{:S(2)}, u32[]{:S(2)}) collective-permute-start(bf16[528,256]{1,0:T(8,128)(2,1)S(1)} %shard_map.86.refs_0_), channel_id=1, source_target_pairs={{0,56},{8,0},{16,8},{24,16},{32,24},{40,32},{48,40},{56,48},{1,57}... | collective-permute-start | bytes 811016 | tf_op jit(solution)/shard_map/ppermute | solution.py:32
  62.6 10.1 %collective-permute-start.5 = (bf16[528,256]{1,0:T(8,128)(2,1)S(1)}, bf16[528,256]{1,0:T(8,128)(2,1)S(1)}, u32[]{:S(2)}, u32[]{:S(2)}) collective-permute-start(bf16[528,256]{1,0:T(8,128)(2,1)S(1)} %shard_map.86.refs_0_), channel_id=1, source_target_pairs={{0,8},{8,16},{16,24},{24,32},{32,40},{40,48},{48,56},{56,0},{1,9},... | collective-permute-start | bytes 811016 | tf_op jit(solution)/shard_map/ppermute | solution.py:32
  68.9 10.4 %collective-permute-start.8 = (bf16[528,256]{1,0:T(8,128)(2,1)S(1)}, bf16[528,256]{1,0:T(8,128)(2,1)S(1)}, u32[]{:S(2)}, u32[]{:S(2)}) collective-permute-start(bf16[528,256]{1,0:T(8,128)(2,1)S(1)} %collective-permute-done.6.refs_2_), channel_id=1, source_target_pairs={{0,56},{8,0},{16,8},{24,16},{32,24},{40,32},{48,40},{56,48},{1,57}... | collective-permute-start | bytes 811016 | tf_op jit(solution)/shard_map/ppermute | solution.py:32
  72.6 9.0 %collective-permute-start.7 = (bf16[528,256]{1,0:T(8,128)(2,1)S(1)}, bf16[528,256]{1,0:T(8,128)(2,1)S(1)}, u32[]{:S(2)}, u32[]{:S(2)}) collective-permute-start(bf16[528,256]{1,0:T(8,128)(2,1)S(1)} %collective-permute-done.5.refs_1_), channel_id=1, source_target_pairs={{0,8},{8,16},{16,24},{24,32},{32,40},{40,48},{48,56},{56,0},{1,9},... | collective-permute-start | bytes 811016 | tf_op jit(solution)/shard_map/ppermute | solution.py:32
  79.3 17.8 %collective-permute-start.12 = (bf16[272,256]{1,0:T(8,128)(2,1)S(1)}, bf16[272,256]{1,0:T(8,128)(2,1)S(1)}, u32[]{:S(2)}, u32[]{:S(2)}) collective-permute-start(bf16[272,256]{1,0:T(8,128)(2,1)S(1)} %slice.81), channel_id=1, source_target_pairs={{0,48},{8,56},{16,0},{24,8},{32,16},{40,24},{48,32},{56,40},{1,49}... | collective-permute-start | bytes 417800 | tf_op jit(solution)/shard_map/ppermute | solution.py:32
  81.6 15.4 %collective-permute-start.11 = (bf16[256,256]{1,0:T(8,128)(2,1)S(1)}, bf16[256,256]{1,0:T(8,128)(2,1)S(1)}, u32[]{:S(2)}, u32[]{:S(2)}) collective-permute-start(bf16[256,256]{1,0:T(8,128)(2,1)S(1)} %slice.80), channel_id=1, source_target_pairs={{0,16},{8,24},{16,32},{24,40},{32,48},{40,56},{48,0},{56,8},{1,17}... | collective-permute-start | bytes 393224 | tf_op jit(solution)/shard_map/ppermute | solution.py:32
  82.4 14.7 %collective-permute-start.10 = (bf16[528,256]{1,0:T(8,128)(2,1)S(1)}, bf16[528,256]{1,0:T(8,128)(2,1)S(1)}, u32[]{:S(2)}, u32[]{:S(2)}) collective-permute-start(bf16[528,256]{1,0:T(8,128)(2,1)S(1)} %collective-permute-done.8.refs_2_), channel_id=1, source_target_pairs={{0,56},{8,0},{16,8},{24,16},{32,24},{40,32},{48,40},{56,48},{1,57}... | collective-permute-start | bytes 811016 | tf_op jit(solution)/shard_map/ppermute | solution.py:32
  88.8 8.4 %collective-permute-start.9 = (bf16[528,256]{1,0:T(8,128)(2,1)S(1)}, bf16[528,256]{1,0:T(8,128)(2,1)S(1)}, u32[]{:S(2)}, u32[]{:S(2)}) collective-permute-start(bf16[528,256]{1,0:T(8,128)(2,1)S(1)} %collective-permute-done.7.refs_1_), channel_id=1, source_target_pairs={{0,8},{8,16},{16,24},{24,32},{32,40},{40,48},{48,56},{56,0},{1,9},... | collective-permute-start | bytes 811016 | tf_op jit(solution)/shard_map/ppermute | solution.py:32
  98.5 10.6 %collective-permute-start.13 = (f32[520,256]{1,0:T(8,128)S(1)}, f32[520,256]{1,0:T(8,128)S(1)}, u32[]{:S(2)}, u32[]{:S(2)}) collective-permute-start(f32[520,256]{1,0:T(8,128)S(1)} %slice.82), channel_id=1, source_target_pairs={{0,4},{4,0},{1,5},{5,1},{2,6},{6,2},{3,7},{7,3},{8,12},{12,8},{9,1... | collective-permute-start | bytes 1597448 | tf_op jit(solution)/shard_map/ppermute | solution.py:36
  117.0 9.1 %collective-permute-start.16 = (bf16[256,256]{1,0:T(8,128)(2,1)S(1)}, bf16[256,256]{1,0:T(8,128)(2,1)S(1)}, u32[]{:S(2)}, u32[]{:S(2)}) collective-permute-start(bf16[256,256]{1,0:T(8,128)(2,1)S(1)} %shard_map.92.own_ref), channel_id=1, source_target_pairs={{0,4},{4,0},{1,5},{5,1},{2,6},{6,2},{3,7},{7,3},{8,12},{12,8},{9,1... | collective-permute-start | bytes 393224 | tf_op jit(solution)/shard_map/ppermute | solution.py:36
  127.2 17.0 %collective-permute-start.19 = (bf16[512,256]{1,0:T(8,128)(2,1)S(1)}, bf16[512,256]{1,0:T(8,128)(2,1)S(1)}, u32[]{:S(2)}, u32[]{:S(2)}) collective-permute-start(bf16[512,256]{1,0:T(8,128)(2,1)S(1)} %get-tuple-element.47), channel_id=1, source_target_pairs={{0,8},{8,16},{16,24},{24,32},{32,40},{40,48},{48,56},{56,0},{1,9},... | collective-permute-start | bytes 786440 | tf_op jit(solution)/shard_map/ppermute | solution.py:32
  132.5 11.8 %collective-permute-start.20 = (bf16[256,256]{1,0:T(8,128)(2,1)S(1)}, bf16[256,256]{1,0:T(8,128)(2,1)S(1)}, u32[]{:S(2)}, u32[]{:S(2)}) collective-permute-start(bf16[256,256]{1,0:T(8,128)(2,1)S(1)} %get-tuple-element.96), channel_id=1, source_target_pairs={{0,16},{8,24},{16,32},{24,40},{32,48},{40,56},{48,0},{56,8},{1,17}... | collective-permute-start | bytes 393224 | tf_op jit(solution)/shard_map/ppermute | solution.py:32
  132.6 12.0 %collective-permute-start.24 = (bf16[256,256]{1,0:T(8,128)(2,1)S(1)}, bf16[256,256]{1,0:T(8,128)(2,1)S(1)}, u32[]{:S(2)}, u32[]{:S(2)}) collective-permute-start(bf16[256,256]{1,0:T(8,128)(2,1)S(1)} %get-tuple-element.97), channel_id=1, source_target_pairs={{0,48},{8,56},{16,0},{24,8},{32,16},{40,24},{48,32},{56,40},{1,49}... | collective-permute-start | bytes 393224 | tf_op jit(solution)/shard_map/ppermute | solution.py:32
  136.7 11.2 %collective-permute-start.23 = (bf16[512,256]{1,0:T(8,128)(2,1)S(1)}, bf16[512,256]{1,0:T(8,128)(2,1)S(1)}, u32[]{:S(2)}, u32[]{:S(2)}) collective-permute-start(bf16[512,256]{1,0:T(8,128)(2,1)S(1)} %get-tuple-element.51), channel_id=1, source_target_pairs={{0,56},{8,0},{16,8},{24,16},{32,24},{40,32},{48,40},{56,48},{1,57}... | collective-permute-start | bytes 786440 | tf_op jit(solution)/shard_map/ppermute | solution.py:32
  144.3 9.6 %collective-permute-start.21 = (bf16[512,256]{1,0:T(8,128)(2,1)S(1)}, bf16[512,256]{1,0:T(8,128)(2,1)S(1)}, u32[]{:S(2)}, u32[]{:S(2)}) collective-permute-start(bf16[512,256]{1,0:T(8,128)(2,1)S(1)} %add_convert_fusion.21), channel_id=1, source_target_pairs={{0,8},{8,16},{16,24},{24,32},{32,40},{40,48},{48,56},{56,0},{1,9},... | collective-permute-start | bytes 786440 | tf_op jit(solution)/shard_map/ppermute | solution.py:32
  148.0 9.1 %collective-permute-start.25 = (bf16[512,256]{1,0:T(8,128)(2,1)S(1)}, bf16[512,256]{1,0:T(8,128)(2,1)S(1)}, u32[]{:S(2)}, u32[]{:S(2)}) collective-permute-start(bf16[512,256]{1,0:T(8,128)(2,1)S(1)} %add_convert_fusion.19), channel_id=1, source_target_pairs={{0,56},{8,0},{16,8},{24,16},{32,24},{40,32},{48,40},{56,48},{1,57}... | collective-permute-start | bytes 786440 | tf_op jit(solution)/shard_map/ppermute | solution.py:32
  151.8 20.1 %collective-permute-start.18 = (bf16[512,256]{1,0:T(8,128)(2,1)S(1)}, bf16[512,256]{1,0:T(8,128)(2,1)S(1)}, u32[]{:S(2)}, u32[]{:S(2)}) collective-permute-start(bf16[512,256]{1,0:T(8,128)(2,1)S(1)} %add_convert_fusion.22), channel_id=1, source_target_pairs={{0,64},{64,128},{128,192},{192,0},{1,65},{65,129},{129,193},{193,1... | collective-permute-start | bytes 786440 | tf_op jit(solution)/shard_map/ppermute | solution.py:41
  154.0 18.0 %collective-permute-start.22 = (bf16[512,256]{1,0:T(8,128)(2,1)S(1)}, bf16[512,256]{1,0:T(8,128)(2,1)S(1)}, u32[]{:S(2)}, u32[]{:S(2)}) collective-permute-start(bf16[512,256]{1,0:T(8,128)(2,1)S(1)} %add_convert_fusion.20), channel_id=1, source_target_pairs={{0,72},{8,80},{16,88},{24,96},{32,104},{40,112},{48,120},{56,64},{... | collective-permute-start | bytes 786440 | tf_op jit(solution)/shard_map/ppermute | solution.py:51
  157.2 14.8 %collective-permute-start.26 = (bf16[512,256]{1,0:T(8,128)(2,1)S(1)}, bf16[512,256]{1,0:T(8,128)(2,1)S(1)}, u32[]{:S(2)}, u32[]{:S(2)}) collective-permute-start(bf16[512,256]{1,0:T(8,128)(2,1)S(1)} %add_convert_fusion.18), channel_id=1, source_target_pairs={{0,120},{8,64},{16,72},{24,80},{32,88},{40,96},{48,104},{56,112},{... | collective-permute-start | bytes 786440 | tf_op jit(solution)/shard_map/ppermute | solution.py:51
  187.0 11.8 %collective-permute-start.32 = (bf16[528,256]{1,0:T(8,128)(2,1)S(1)}, bf16[528,256]{1,0:T(8,128)(2,1)S(1)}, u32[]{:S(2)}, u32[]{:S(2)}) collective-permute-start(bf16[528,256]{1,0:T(8,128)(2,1)S(1)} %collective-permute-done.30.refs_2_), channel_id=1, source_target_pairs={{0,56},{8,0},{16,8},{24,16},{32,24},{40,32},{48,40},{56,48},{1,57}... | collective-permute-start | bytes 811016 | tf_op jit(solution)/shard_map/ppermute | solution.py:32
  188.8 10.0 %collective-permute-start.31 = (bf16[528,256]{1,0:T(8,128)(2,1)S(1)}, bf16[528,256]{1,0:T(8,128)(2,1)S(1)}, u32[]{:S(2)}, u32[]{:S(2)}) collective-permute-start(bf16[528,256]{1,0:T(8,128)(2,1)S(1)} %collective-permute-done.29.refs_1_), channel_id=1, source_target_pairs={{0,8},{8,16},{16,24},{24,32},{32,40},{40,48},{48,56},{56,0},{1,9},... | collective-permute-start | bytes 811016 | tf_op jit(solution)/shard_map/ppermute | solution.py:32
  189.0 9.7 %collective-permute-start.34 = (bf16[272,256]{1,0:T(8,128)(2,1)S(1)}, bf16[272,256]{1,0:T(8,128)(2,1)S(1)}, u32[]{:S(2)}, u32[]{:S(2)}) collective-permute-start(bf16[272,256]{1,0:T(8,128)(2,1)S(1)} %slice.84), channel_id=1, source_target_pairs={{0,48},{8,56},{16,0},{24,8},{32,16},{40,24},{48,32},{56,40},{1,49}... | collective-permute-start | bytes 417800 | tf_op jit(solution)/shard_map/ppermute | solution.py:32
  218.1 17.1 %collective-permute-start.40 = (bf16[512,256]{1,0:T(8,128)(2,1)S(1)}, bf16[512,256]{1,0:T(8,128)(2,1)S(1)}, u32[]{:S(2)}, u32[]{:S(2)}) collective-permute-start(bf16[512,256]{1,0:T(8,128)(2,1)S(1)} %get-tuple-element.57), channel_id=1, source_target_pairs={{0,8},{8,16},{16,24},{24,32},{32,40},{40,48},{48,56},{56,0},{1,9},... | collective-permute-start | bytes 786440 | tf_op jit(solution)/shard_map/ppermute | solution.py:32
  223.7 11.5 %collective-permute-start.41 = (bf16[256,256]{1,0:T(8,128)(2,1)S(1)}, bf16[256,256]{1,0:T(8,128)(2,1)S(1)}, u32[]{:S(2)}, u32[]{:S(2)}) collective-permute-start(bf16[256,256]{1,0:T(8,128)(2,1)S(1)} %get-tuple-element.94), channel_id=1, source_target_pairs={{0,16},{8,24},{16,32},{24,40},{32,48},{40,56},{48,0},{56,8},{1,17}... | collective-permute-start | bytes 393224 | tf_op jit(solution)/shard_map/ppermute | solution.py:32
  224.2 11.6 %collective-permute-start.45 = (bf16[256,256]{1,0:T(8,128)(2,1)S(1)}, bf16[256,256]{1,0:T(8,128)(2,1)S(1)}, u32[]{:S(2)}, u32[]{:S(2)}) collective-permute-start(bf16[256,256]{1,0:T(8,128)(2,1)S(1)} %get-tuple-element.95), channel_id=1, source_target_pairs={{0,48},{8,56},{16,0},{24,8},{32,16},{40,24},{48,32},{56,40},{1,49}... | collective-permute-start | bytes 393224 | tf_op jit(solution)/shard_map/ppermute | solution.py:32
  228.4 10.9 %collective-permute-start.44 = (bf16[512,256]{1,0:T(8,128)(2,1)S(1)}, bf16[512,256]{1,0:T(8,128)(2,1)S(1)}, u32[]{:S(2)}, u32[]{:S(2)}) collective-permute-start(bf16[512,256]{1,0:T(8,128)(2,1)S(1)} %get-tuple-element.61), channel_id=1, source_target_pairs={{0,56},{8,0},{16,8},{24,16},{32,24},{40,32},{48,40},{56,48},{1,57}... | collective-permute-start | bytes 786440 | tf_op jit(solution)/shard_map/ppermute | solution.py:32
  235.3 9.9 %collective-permute-start.42 = (bf16[512,256]{1,0:T(8,128)(2,1)S(1)}, bf16[512,256]{1,0:T(8,128)(2,1)S(1)}, u32[]{:S(2)}, u32[]{:S(2)}) collective-permute-start(bf16[512,256]{1,0:T(8,128)(2,1)S(1)} %add_convert_fusion.15), channel_id=1, source_target_pairs={{0,8},{8,16},{16,24},{24,32},{32,40},{40,48},{48,56},{56,0},{1,9},... | collective-permute-start | bytes 786440 | tf_op jit(solution)/shard_map/ppermute | solution.py:32
  239.3 9.4 %collective-permute-start.46 = (bf16[512,256]{1,0:T(8,128)(2,1)S(1)}, bf16[512,256]{1,0:T(8,128)(2,1)S(1)}, u32[]{:S(2)}, u32[]{:S(2)}) collective-permute-start(bf16[512,256]{1,0:T(8,128)(2,1)S(1)} %add_convert_fusion.13), channel_id=1, source_target_pairs={{0,56},{8,0},{16,8},{24,16},{32,24},{40,32},{48,40},{56,48},{1,57}... | collective-permute-start | bytes 786440 | tf_op jit(solution)/shard_map/ppermute | solution.py:32
  243.2 20.3 %collective-permute-start.39 = (bf16[512,256]{1,0:T(8,128)(2,1)S(1)}, bf16[512,256]{1,0:T(8,128)(2,1)S(1)}, u32[]{:S(2)}, u32[]{:S(2)}) collective-permute-start(bf16[512,256]{1,0:T(8,128)(2,1)S(1)} %add_convert_fusion.16), channel_id=1, source_target_pairs={{0,64},{64,128},{128,192},{192,0},{1,65},{65,129},{129,193},{193,1... | collective-permute-start | bytes 786440 | tf_op jit(solution)/shard_map/ppermute | solution.py:41
  245.2 18.3 %collective-permute-start.43 = (bf16[512,256]{1,0:T(8,128)(2,1)S(1)}, bf16[512,256]{1,0:T(8,128)(2,1)S(1)}, u32[]{:S(2)}, u32[]{:S(2)}) collective-permute-start(bf16[512,256]{1,0:T(8,128)(2,1)S(1)} %add_convert_fusion.14), channel_id=1, source_target_pairs={{0,72},{8,80},{16,88},{24,96},{32,104},{40,112},{48,120},{56,64},{... | collective-permute-start | bytes 786440 | tf_op jit(solution)/shard_map/ppermute | solution.py:51
  248.7 14.7 %collective-permute-start.47 = (bf16[512,256]{1,0:T(8,128)(2,1)S(1)}, bf16[512,256]{1,0:T(8,128)(2,1)S(1)}, u32[]{:S(2)}, u32[]{:S(2)}) collective-permute-start(bf16[512,256]{1,0:T(8,128)(2,1)S(1)} %add_convert_fusion.12), channel_id=1, source_target_pairs={{0,120},{8,64},{16,72},{24,80},{32,88},{40,96},{48,104},{56,112},{... | collective-permute-start | bytes 786440 | tf_op jit(solution)/shard_map/ppermute | solution.py:51
  278.5 15.4 %collective-permute-start.53 = (bf16[528,256]{1,0:T(8,128)(2,1)S(1)}, bf16[528,256]{1,0:T(8,128)(2,1)S(1)}, u32[]{:S(2)}, u32[]{:S(2)}) collective-permute-start(bf16[528,256]{1,0:T(8,128)(2,1)S(1)} %collective-permute-done.51.refs_2_), channel_id=1, source_target_pairs={{0,56},{8,0},{16,8},{24,16},{32,24},{40,32},{48,40},{56,48},{1,57}... | collective-permute-start | bytes 811016 | tf_op jit(solution)/shard_map/ppermute | solution.py:32
  280.5 13.4 %collective-permute-start.52 = (bf16[528,256]{1,0:T(8,128)(2,1)S(1)}, bf16[528,256]{1,0:T(8,128)(2,1)S(1)}, u32[]{:S(2)}, u32[]{:S(2)}) collective-permute-start(bf16[528,256]{1,0:T(8,128)(2,1)S(1)} %collective-permute-done.50.refs_1_), channel_id=1, source_target_pairs={{0,8},{8,16},{16,24},{24,32},{32,40},{40,48},{48,56},{56,0},{1,9},... | collective-permute-start | bytes 811016 | tf_op jit(solution)/shard_map/ppermute | solution.py:32
  280.6 13.3 %collective-permute-start.55 = (bf16[272,256]{1,0:T(8,128)(2,1)S(1)}, bf16[272,256]{1,0:T(8,128)(2,1)S(1)}, u32[]{:S(2)}, u32[]{:S(2)}) collective-permute-start(bf16[272,256]{1,0:T(8,128)(2,1)S(1)} %slice.87), channel_id=1, source_target_pairs={{0,48},{8,56},{16,0},{24,8},{32,16},{40,24},{48,32},{56,40},{1,49}... | collective-permute-start | bytes 417800 | tf_op jit(solution)/shard_map/ppermute | solution.py:32
  285.1 8.8 %collective-permute-start.54 = (bf16[256,256]{1,0:T(8,128)(2,1)S(1)}, bf16[256,256]{1,0:T(8,128)(2,1)S(1)}, u32[]{:S(2)}, u32[]{:S(2)}) collective-permute-start(bf16[256,256]{1,0:T(8,128)(2,1)S(1)} %slice.86), channel_id=1, source_target_pairs={{0,16},{8,24},{16,32},{24,40},{32,48},{40,56},{48,0},{56,8},{1,17}... | collective-permute-start | bytes 393224 | tf_op jit(solution)/shard_map/ppermute | solution.py:32
  311.8 16.4 %collective-permute-start.61 = (bf16[512,256]{1,0:T(8,128)(2,1)S(1)}, bf16[512,256]{1,0:T(8,128)(2,1)S(1)}, u32[]{:S(2)}, u32[]{:S(2)}) collective-permute-start(bf16[512,256]{1,0:T(8,128)(2,1)S(1)} %get-tuple-element.67), channel_id=1, source_target_pairs={{0,8},{8,16},{16,24},{24,32},{32,40},{40,48},{48,56},{56,0},{1,9},... | collective-permute-start | bytes 786440 | tf_op jit(solution)/shard_map/ppermute | solution.py:32
  316.6 11.5 %collective-permute-start.62 = (bf16[256,256]{1,0:T(8,128)(2,1)S(1)}, bf16[256,256]{1,0:T(8,128)(2,1)S(1)}, u32[]{:S(2)}, u32[]{:S(2)}) collective-permute-start(bf16[256,256]{1,0:T(8,128)(2,1)S(1)} %get-tuple-element.92), channel_id=1, source_target_pairs={{0,16},{8,24},{16,32},{24,40},{32,48},{40,56},{48,0},{56,8},{1,17}... | collective-permute-start | bytes 393224 | tf_op jit(solution)/shard_map/ppermute | solution.py:32
  316.7 12.3 %collective-permute-start.66 = (bf16[256,256]{1,0:T(8,128)(2,1)S(1)}, bf16[256,256]{1,0:T(8,128)(2,1)S(1)}, u32[]{:S(2)}, u32[]{:S(2)}) collective-permute-start(bf16[256,256]{1,0:T(8,128)(2,1)S(1)} %get-tuple-element.93), channel_id=1, source_target_pairs={{0,48},{8,56},{16,0},{24,8},{32,16},{40,24},{48,32},{56,40},{1,49}... | collective-permute-start | bytes 393224 | tf_op jit(solution)/shard_map/ppermute | solution.py:32
  320.9 11.2 %collective-permute-start.65 = (bf16[512,256]{1,0:T(8,128)(2,1)S(1)}, bf16[512,256]{1,0:T(8,128)(2,1)S(1)}, u32[]{:S(2)}, u32[]{:S(2)}) collective-permute-start(bf16[512,256]{1,0:T(8,128)(2,1)S(1)} %get-tuple-element.71), channel_id=1, source_target_pairs={{0,56},{8,0},{16,8},{24,16},{32,24},{40,32},{48,40},{56,48},{1,57}... | collective-permute-start | bytes 786440 | tf_op jit(solution)/shard_map/ppermute | solution.py:32
  328.2 9.0 %collective-permute-start.63 = (bf16[512,256]{1,0:T(8,128)(2,1)S(1)}, bf16[512,256]{1,0:T(8,128)(2,1)S(1)}, u32[]{:S(2)}, u32[]{:S(2)}) collective-permute-start(bf16[512,256]{1,0:T(8,128)(2,1)S(1)} %add_convert_fusion.9), channel_id=1, source_target_pairs={{0,8},{8,16},{16,24},{24,32},{32,40},{40,48},{48,56},{56,0},{1,9},... | collective-permute-start | bytes 786440 | tf_op jit(solution)/shard_map/ppermute | solution.py:32
  335.4 19.4 %collective-permute-start.60 = (bf16[512,256]{1,0:T(8,128)(2,1)S(1)}, bf16[512,256]{1,0:T(8,128)(2,1)S(1)}, u32[]{:S(2)}, u32[]{:S(2)}) collective-permute-start(bf16[512,256]{1,0:T(8,128)(2,1)S(1)} %add_convert_fusion.10), channel_id=1, source_target_pairs={{0,64},{64,128},{128,192},{192,0},{1,65},{65,129},{129,193},{193,1... | collective-permute-start | bytes 786440 | tf_op jit(solution)/shard_map/ppermute | solution.py:41
  337.2 17.5 %collective-permute-start.64 = (bf16[512,256]{1,0:T(8,128)(2,1)S(1)}, bf16[512,256]{1,0:T(8,128)(2,1)S(1)}, u32[]{:S(2)}, u32[]{:S(2)}) collective-permute-start(bf16[512,256]{1,0:T(8,128)(2,1)S(1)} %add_convert_fusion.8), channel_id=1, source_target_pairs={{0,72},{8,80},{16,88},{24,96},{32,104},{40,112},{48,120},{56,64},{... | collective-permute-start | bytes 786440 | tf_op jit(solution)/shard_map/ppermute | solution.py:51
  340.1 14.7 %collective-permute-start.68 = (bf16[512,256]{1,0:T(8,128)(2,1)S(1)}, bf16[512,256]{1,0:T(8,128)(2,1)S(1)}, u32[]{:S(2)}, u32[]{:S(2)}) collective-permute-start(bf16[512,256]{1,0:T(8,128)(2,1)S(1)} %add_convert_fusion.6), channel_id=1, source_target_pairs={{0,120},{8,64},{16,72},{24,80},{32,88},{40,96},{48,104},{56,112},{... | collective-permute-start | bytes 786440 | tf_op jit(solution)/shard_map/ppermute | solution.py:51
  355.6 8.5 %collective-permute-start.70 = (bf16[528,256]{1,0:T(8,128)(2,1)S(1)}, bf16[528,256]{1,0:T(8,128)(2,1)S(1)}, u32[]{:S(2)}, u32[]{:S(2)}) collective-permute-start(bf16[528,256]{1,0:T(8,128)(2,1)S(1)} %shard_map.113.refs_0_), channel_id=1, source_target_pairs={{0,56},{8,0},{16,8},{24,16},{32,24},{40,32},{48,40},{56,48},{1,57}... | collective-permute-start | bytes 811016 | tf_op jit(solution)/shard_map/ppermute | solution.py:32
  356.2 8.4 %collective-permute-start.69 = (bf16[528,256]{1,0:T(8,128)(2,1)S(1)}, bf16[528,256]{1,0:T(8,128)(2,1)S(1)}, u32[]{:S(2)}, u32[]{:S(2)}) collective-permute-start(bf16[528,256]{1,0:T(8,128)(2,1)S(1)} %shard_map.113.refs_0_), channel_id=1, source_target_pairs={{0,8},{8,16},{16,24},{24,32},{32,40},{40,48},{48,56},{56,0},{1,9},... | collective-permute-start | bytes 811016 | tf_op jit(solution)/shard_map/ppermute | solution.py:32
  364.1 9.3 %collective-permute-start.72 = (bf16[528,256]{1,0:T(8,128)(2,1)S(1)}, bf16[528,256]{1,0:T(8,128)(2,1)S(1)}, u32[]{:S(2)}, u32[]{:S(2)}) collective-permute-start(bf16[528,256]{1,0:T(8,128)(2,1)S(1)} %collective-permute-done.70.refs_2_), channel_id=1, source_target_pairs={{0,56},{8,0},{16,8},{24,16},{32,24},{40,32},{48,40},{56,48},{1,57}... | collective-permute-start | bytes 811016 | tf_op jit(solution)/shard_map/ppermute | solution.py:32
  364.6 11.0 %collective-permute-start.71 = (bf16[528,256]{1,0:T(8,128)(2,1)S(1)}, bf16[528,256]{1,0:T(8,128)(2,1)S(1)}, u32[]{:S(2)}, u32[]{:S(2)}) collective-permute-start(bf16[528,256]{1,0:T(8,128)(2,1)S(1)} %collective-permute-done.69.refs_1_), channel_id=1, source_target_pairs={{0,8},{8,16},{16,24},{24,32},{32,40},{40,48},{48,56},{56,0},{1,9},... | collective-permute-start | bytes 811016 | tf_op jit(solution)/shard_map/ppermute | solution.py:32
  373.4 11.3 %collective-permute-start.74 = (bf16[528,256]{1,0:T(8,128)(2,1)S(1)}, bf16[528,256]{1,0:T(8,128)(2,1)S(1)}, u32[]{:S(2)}, u32[]{:S(2)}) collective-permute-start(bf16[528,256]{1,0:T(8,128)(2,1)S(1)} %collective-permute-done.72.refs_2_), channel_id=1, source_target_pairs={{0,56},{8,0},{16,8},{24,16},{32,24},{40,32},{48,40},{56,48},{1,57}... | collective-permute-start | bytes 811016 | tf_op jit(solution)/shard_map/ppermute | solution.py:32
  375.6 9.1 %collective-permute-start.73 = (bf16[528,256]{1,0:T(8,128)(2,1)S(1)}, bf16[528,256]{1,0:T(8,128)(2,1)S(1)}, u32[]{:S(2)}, u32[]{:S(2)}) collective-permute-start(bf16[528,256]{1,0:T(8,128)(2,1)S(1)} %collective-permute-done.71.refs_1_), channel_id=1, source_target_pairs={{0,8},{8,16},{16,24},{24,32},{32,40},{40,48},{48,56},{56,0},{1,9},... | collective-permute-start | bytes 811016 | tf_op jit(solution)/shard_map/ppermute | solution.py:32
  375.6 9.0 %collective-permute-start.76 = (bf16[272,256]{1,0:T(8,128)(2,1)S(1)}, bf16[272,256]{1,0:T(8,128)(2,1)S(1)}, u32[]{:S(2)}, u32[]{:S(2)}) collective-permute-start(bf16[272,256]{1,0:T(8,128)(2,1)S(1)} %slice.90), channel_id=1, source_target_pairs={{0,48},{8,56},{16,0},{24,8},{32,16},{40,24},{48,32},{56,40},{1,49}... | collective-permute-start | bytes 417800 | tf_op jit(solution)/shard_map/ppermute | solution.py:32
  405.1 17.6 %collective-permute-start.81 = (bf16[512,256]{1,0:T(8,128)(2,1)S(1)}, bf16[512,256]{1,0:T(8,128)(2,1)S(1)}, u32[]{:S(2)}, u32[]{:S(2)}) collective-permute-start(bf16[512,256]{1,0:T(8,128)(2,1)S(1)} %get-tuple-element.77), channel_id=1, source_target_pairs={{0,8},{8,16},{16,24},{24,32},{32,40},{40,48},{48,56},{56,0},{1,9},... | collective-permute-start | bytes 786440 | tf_op jit(solution)/shard_map/ppermute | solution.py:32
  411.3 11.5 %collective-permute-start.82 = (bf16[256,256]{1,0:T(8,128)(2,1)S(1)}, bf16[256,256]{1,0:T(8,128)(2,1)S(1)}, u32[]{:S(2)}, u32[]{:S(2)}) collective-permute-start(bf16[256,256]{1,0:T(8,128)(2,1)S(1)} %get-tuple-element.90), channel_id=1, source_target_pairs={{0,16},{8,24},{16,32},{24,40},{32,48},{40,56},{48,0},{56,8},{1,17}... | collective-permute-start | bytes 393224 | tf_op jit(solution)/shard_map/ppermute | solution.py:32
  411.4 12.0 %collective-permute-start.86 = (bf16[256,256]{1,0:T(8,128)(2,1)S(1)}, bf16[256,256]{1,0:T(8,128)(2,1)S(1)}, u32[]{:S(2)}, u32[]{:S(2)}) collective-permute-start(bf16[256,256]{1,0:T(8,128)(2,1)S(1)} %get-tuple-element.91), channel_id=1, source_target_pairs={{0,48},{8,56},{16,0},{24,8},{32,16},{40,24},{48,32},{56,40},{1,49}... | collective-permute-start | bytes 393224 | tf_op jit(solution)/shard_map/ppermute | solution.py:32
  415.5 10.9 %collective-permute-start.85 = (bf16[512,256]{1,0:T(8,128)(2,1)S(1)}, bf16[512,256]{1,0:T(8,128)(2,1)S(1)}, u32[]{:S(2)}, u32[]{:S(2)}) collective-permute-start(bf16[512,256]{1,0:T(8,128)(2,1)S(1)} %get-tuple-element.81), channel_id=1, source_target_pairs={{0,56},{8,0},{16,8},{24,16},{32,24},{40,32},{48,40},{56,48},{1,57}... | collective-permute-start | bytes 786440 | tf_op jit(solution)/shard_map/ppermute | solution.py:32
  422.8 10.6 %collective-permute-start.83 = (bf16[512,256]{1,0:T(8,128)(2,1)S(1)}, bf16[512,256]{1,0:T(8,128)(2,1)S(1)}, u32[]{:S(2)}, u32[]{:S(2)}) collective-permute-start(bf16[512,256]{1,0:T(8,128)(2,1)S(1)} %add_convert_fusion.4), channel_id=1, source_target_pairs={{0,8},{8,16},{16,24},{24,32},{32,40},{40,48},{48,56},{56,0},{1,9},... | collective-permute-start | bytes 786440 | tf_op jit(solution)/shard_map/ppermute | solution.py:32
  426.4 9.0 %collective-permute-start.87 = (bf16[512,256]{1,0:T(8,128)(2,1)S(1)}, bf16[512,256]{1,0:T(8,128)(2,1)S(1)}, u32[]{:S(2)}, u32[]{:S(2)}) collective-permute-start(bf16[512,256]{1,0:T(8,128)(2,1)S(1)} %add_convert_fusion.2), channel_id=1, source_target_pairs={{0,56},{8,0},{16,8},{24,16},{32,24},{40,32},{48,40},{56,48},{1,57}... | collective-permute-start | bytes 786440 | tf_op jit(solution)/shard_map/ppermute | solution.py:32
  430.2 9.0 %collective-permute-start.90 = (bf16[512,256]{1,0:T(8,128)(2,1)S(1)}, bf16[512,256]{1,0:T(8,128)(2,1)S(1)}, u32[]{:S(2)}, u32[]{:S(2)}) collective-permute-start(bf16[512,256]{1,0:T(8,128)(2,1)S(1)} %get-tuple-element.82), channel_id=1, source_target_pairs={{0,192},{64,128},{128,64},{192,0},{1,193},{65,129},{129,65},{193,1... | collective-permute-start | bytes 786440 | tf_op jit(solution)/shard_map/ppermute | solution.py:352
  430.2 10.8 %collective-permute-start.89 = (bf16[512,256]{1,0:T(8,128)(2,1)S(1)}, bf16[512,256]{1,0:T(8,128)(2,1)S(1)}, u32[]{:S(2)}, u32[]{:S(2)}) collective-permute-start(bf16[512,256]{1,0:T(8,128)(2,1)S(1)} %get-tuple-element.82), channel_id=1, source_target_pairs={{0,192},{64,0},{128,64},{192,128},{1,193},{65,1},{129,65},{193,129... | collective-permute-start | bytes 786440 | tf_op jit(solution)/shard_map/ppermute | solution.py:41
  (39 other events, 566.1 us)
